TPU v7x, 32 devices: a whole 2x2x4 slice. The times are simulated.
32 devices in a mesh: ang: 4 (over y, x), pul: 8 (over z, core).
Axes of the slice: x: 2, y: 2, z: 4, core: 2. Of those that a mesh axis runs over, the one named last changes fastest.
Arguments:
- pulses: bfloat16 [2, 1024, 16384], P(None, ('ang', 'pul')), may hold values from -6 to 6
- matched_filter: float32 [2, 16384], replicated, may hold values from -6 to 6
- interp_weights: bfloat16 [4, 8, 64, 256], P('ang', 'pul'), may hold values from -0.75 to 0.75
- offsets: int32 [4, 8, 8], P('ang', 'pul'), may hold values from 0 to 192, as said below
Outputs:
- image: float32 [32, 2, 2048], P(('ang', 'pul'))
Inputs may be any that keep to these rules, and one draw needn't show every extreme that they name: `offsets`: each block's window of 64 pulses lies inside its group; the first block of every tile starts at 0 and the last at 192.
All inputs are finite; a program needn't handle non-finite values.
Results may differ from a plain program's by a relative error of at most 0.015.
Values may be sent and summed in bfloat16 or wider, within the bound.
No kernel may reach another device: no remote copies, remote signals or barrier semaphores. Data moves between devices by JAX's collectives and lax.ppermute only.
A program may use at most 64 MiB of HBM per device.

v0:
```python
import math

import jax
import jax.numpy as jnp
from jax import lax
from jax.sharding import PartitionSpec as P

FACTOR = 128
BLOCK_ROWS = 32
BAND_PULSES = 64
ROWS_DEV = 1
IMAGE_COLS = 2048


HIGHEST_MODE = lax.Precision.HIGHEST


def small_tables(length, sign):
    places = jnp.arange(length, dtype=jnp.int32)
    phase = jnp.mod(places[:, None] * places[None, :], length)
    angle = phase.astype(jnp.float32) * (sign * 2.0 * math.pi / length)
    return (jnp.cos(angle), jnp.sin(angle))


def twiddles(factor, sign):
    places = jnp.arange(factor, dtype=jnp.int32)
    phase = jnp.mod(places[:, None] * places[None, :], factor * factor)
    angle = phase.astype(jnp.float32) * (sign * 2.0 * math.pi / (factor * factor))
    return (jnp.cos(angle), jnp.sin(angle))


def range_forward(real_part, imag_part, factor):
    row_total = real_part.shape[0]
    cos_full, sin_full = small_tables(factor, -1.0)
    cos_small = cos_full.astype(jnp.bfloat16)
    sin_small = sin_full.astype(jnp.bfloat16)
    twist_cos, twist_sin = twiddles(factor, -1.0)
    real_grid = real_part.reshape(row_total, factor, factor)
    imag_grid = imag_part.reshape(row_total, factor, factor)
    section_real = jnp.einsum(
        "km,rmn->rkn", cos_small, real_grid, preferred_element_type=jnp.float32
    ) - jnp.einsum("km,rmn->rkn", sin_small, imag_grid, preferred_element_type=jnp.float32)
    section_imag = jnp.einsum(
        "km,rmn->rkn", cos_small, imag_grid, preferred_element_type=jnp.float32
    ) + jnp.einsum("km,rmn->rkn", sin_small, real_grid, preferred_element_type=jnp.float32)
    turned_real = (section_real * twist_cos - section_imag * twist_sin).astype(jnp.bfloat16)
    turned_imag = (section_real * twist_sin + section_imag * twist_cos).astype(jnp.bfloat16)
    final_real = jnp.einsum(
        "rkm,mj->rkj", turned_real, cos_small, preferred_element_type=jnp.float32
    ) - jnp.einsum("rkm,mj->rkj", turned_imag, sin_small, preferred_element_type=jnp.float32)
    final_imag = jnp.einsum(
        "rkm,mj->rkj", turned_real, sin_small, preferred_element_type=jnp.float32
    ) + jnp.einsum("rkm,mj->rkj", turned_imag, cos_small, preferred_element_type=jnp.float32)
    length = factor * factor
    return (
        jnp.transpose(final_real, (0, 2, 1)).reshape(row_total, length),
        jnp.transpose(final_imag, (0, 2, 1)).reshape(row_total, length),
    )


def local(pulses, matched_filter, interp_weights, offsets):
    pul_count = lax.axis_size("pul")
    ang_count = lax.axis_size("ang")
    group_index = lax.axis_index("ang")
    member_index = lax.axis_index("pul")
    range_bins = pulses.shape[2]
    bins_tile = range_bins // pul_count
    group_pulses = pulses.shape[1] * pul_count
    total_rows = group_pulses * ang_count
    image_rows = ROWS_DEV * ang_count * pul_count
    first_column = (range_bins - IMAGE_COLS) // 2
    root_bins = math.sqrt(range_bins)
    wave_real, wave_imag = range_forward(pulses[0], pulses[1], FACTOR)
    wave_real = wave_real / root_bins
    wave_imag = wave_imag / root_bins
    spec_real = wave_real * matched_filter[0] - wave_imag * matched_filter[1]
    spec_imag = wave_real * matched_filter[1] + wave_imag * matched_filter[0]
    spectrum = jnp.stack([spec_real, spec_imag]).astype(jnp.bfloat16)
    arranged = spectrum.reshape(2, pulses.shape[1], pul_count, bins_tile)
    block_starts = offsets[0, 0]
    kernel = interp_weights[0, 0].reshape(BAND_PULSES, -1, BLOCK_ROWS)
    panel = lax.all_to_all(arranged, "pul", split_axis=2, concat_axis=1, tiled=True)[:, :, 0, :]
    windows = jax.vmap(
        lambda begin_pulse: lax.dynamic_slice_in_dim(panel, begin_pulse, BAND_PULSES, 1)
    )(block_starts)
    mixed = jnp.einsum("jbk,bcjn->cbkn", kernel, windows, preferred_element_type=jnp.float32)
    resampled = mixed.reshape(2, panel.shape[1], panel.shape[2]).astype(jnp.bfloat16)
    stacked = resampled.reshape(2 * group_pulses, bins_tile)
    grid_rows = group_index * group_pulses + jnp.arange(group_pulses, dtype=jnp.int32)
    image_index = jnp.arange(pul_count * ROWS_DEV * lax.axis_size("ang"), dtype=jnp.int32)
    phase = jnp.mod((image_index[:, None] - image_rows // 2) * grid_rows[None, :], total_rows)
    angle = phase.astype(jnp.float32) * (2.0 * math.pi / total_rows)
    table_real = (jnp.cos(angle) / math.sqrt(total_rows)).astype(jnp.bfloat16)
    table_imag = (jnp.sin(angle) / math.sqrt(total_rows)).astype(jnp.bfloat16)
    real_rows = jnp.concatenate([table_real, -table_imag], axis=1)
    imag_rows = jnp.concatenate([table_imag, table_real], axis=1)
    combined = jnp.stack([real_rows, imag_rows], axis=1).reshape(
        pul_count * ROWS_DEV * lax.axis_size("ang") * 2, 2 * group_pulses
    )
    product = jnp.dot(combined, stacked, preferred_element_type=jnp.float32)
    summed = lax.psum_scatter(
        product.reshape(pul_count * ROWS_DEV * lax.axis_size("ang"), 2, bins_tile)
        .astype(jnp.bfloat16)
        .astype(jnp.float32)
        .astype(jnp.bfloat16),
        "ang",
        scatter_dimension=0,
        tiled=True,
    ).astype(jnp.float32)
    tile_bins = member_index * bins_tile + jnp.arange(bins_tile, dtype=jnp.int32)
    columns_index = first_column + jnp.arange(IMAGE_COLS, dtype=jnp.int32)
    range_phase = jnp.mod(tile_bins[:, None] * columns_index[None, :], range_bins)
    range_angle = range_phase.astype(jnp.float32) * (2.0 * math.pi / range_bins)
    range_cos = jnp.cos(range_angle) / root_bins
    range_sin = jnp.sin(range_angle) / root_bins
    part_real = jnp.dot(summed[:, 0], range_cos, precision=HIGHEST_MODE) - jnp.dot(
        summed[:, 1], range_sin, precision=HIGHEST_MODE
    )
    part_imag = jnp.dot(summed[:, 0], range_sin, precision=HIGHEST_MODE) + jnp.dot(
        summed[:, 1], range_cos, precision=HIGHEST_MODE
    )
    return lax.psum_scatter(
        jnp.stack([part_real, part_imag], axis=1).astype(jnp.bfloat16),
        "pul",
        scatter_dimension=0,
        tiled=True,
    ).astype(jnp.float32)


def solution(mesh):
    placed = (
        P(None, ("ang", "pul"), None),
        P(),
        P("ang", "pul", None, None),
        P("ang", "pul", None),
    )
    return jax.shard_map(
        local, mesh=mesh, in_specs=placed, out_specs=P(("ang", "pul"), None, None), check_vma=False
    )
```

profile of v0, /device:TPU:0, one launch (start us, length us, event | category | flops | bytes accessed | tf_op | source)
XLA Modules:
  0.0 495.3 jit_solution(11746952005725622309)
XLA Ops:
  6.8 1.7 slice_bitcast_fusion.1
  8.8 0.6 fusion.53
  9.6 0.6 fusion.55
  10.3 0.6 convolution_add_fusion
  10.9 1.1 fusion.23
  12.0 0.7 fusion.51
  12.7 2.0 fusion.45
  14.7 0.7 subtract_bitcast_fusion
  15.3 1.8 copy.18
  17.2 1.7 reshape.219
  18.9 3.6 add_bitcast_fusion
  22.5 2.9 copy.19
  25.4 2.7 reshape.220
  28.1 0.4 multiply_reduce_fusion.1
  28.6 2.2 subtract_convert_fusion
  31.0 2.5 copy.20
  33.5 6.3 %all-to-all-start = ((bf16[2,32,8,2048]{3,1,0,2:T(8,128)(2,1)}), bf16[2,32,8,2048]{3,1,0,2:T(8,128)(2,1)}, u32[]{:S(2)}, u32[]{:S(2)}) async-start(bf16[2,32,8,2048]{3,1,0,2:T(8,128)(2,1)} %copy.20), calls=%async_computation | async-start | bytes 4194304 | tf_op jit(solution)/shard_map/all_to_all | solution.py:82
  40.5 48.5 %all-to-all-done = bf16[2,32,8,2048]{3,1,0,2:T(8,128)(2,1)} async-done(((bf16[2,32,8,2048]{3,1,0,2:T(8,128)(2,1)}), bf16[2,32,8,2048]{3,1,0,2:T(8,128)(2,1)}, u32[]{:S(2)}, u32[]{:S(2)}) %all-to-all-start) | async-done | bytes 2097184 | tf_op jit(solution)/shard_map/all_to_all | solution.py:82
  89.0 1.7 copy.21
  90.7 18.2 %while.1 = (s32[]{:T(128)}, bf16[2,256,2048]{2,1,0:T(8,128)(2,1)S(1)}, s32[8,3]{0,1:T(4,128)S(1)}, bf16[8,2,64,2048]{3,2,1,0:T(8,128)(2,1)}, s32[]{:T(128)}) while((s32[]{:T(128)}, bf16[2,256,2048]{2,1,0:T(8,128)(2,1)S(1)}, s32[8,3]{0,1:T(4,128)S(1)}, bf16[8,2,64,2048]{3,2,1,0:T(8,128)(2,1)}, s32[]{:T(128)}) %tuple.31), condition=%wide.while_cond, body=%wide.while_body.sunk | while | flops 2 | bytes 1049697 | solution.py:84
  90.8 0.6 slice.48
  91.4 1.6 bitcast_dynamic-update-slice_fusion.2
  93.0 0.6 slice.48
  93.6 1.6 bitcast_dynamic-update-slice_fusion.2
  95.3 0.6 slice.48
  95.9 1.6 bitcast_dynamic-update-slice_fusion.2
  97.6 0.6 slice.48
  98.2 1.6 bitcast_dynamic-update-slice_fusion.2
  99.9 0.6 slice.48
  100.4 1.6 bitcast_dynamic-update-slice_fusion.2
  102.1 0.6 slice.48
  102.7 1.6 bitcast_dynamic-update-slice_fusion.2
  104.4 0.6 slice.48
  105.0 1.6 bitcast_dynamic-update-slice_fusion.2
  106.7 0.6 slice.48
  107.2 1.6 bitcast_dynamic-update-slice_fusion.2
  108.8 2.9 fusion.15
  112.0 1.2 convolution_convert_fusion.1
  113.5 0.6 dynamic-slice.4
  114.8 40.4 %all-reduce.5.cloned.1.call-done = bf16[32,2,2048]{2,0,1:T(8,128)(2,1)} async-done(((bf16[32,2,2048]{2,0,1:T(8,128)(2,1)}), bf16[32,2,2048]{2,0,1:T(8,128)(2,1)}) %all-reduce.5.cloned.1.call-update) | async-done | bytes 262160
  155.2 68.7 %fusion.4 = f32[8,2048]{1,0:T(8,128)S(1)} fusion(s32[2048]{0:T(1024)S(1)} %get-tuple-element.35, s32[2048]{0:T(1024)S(1)} %get-tuple-element.36, bf16[32,2,2048]{2,0,1:T(8,128)(2,1)} %all-reduce.5.cloned.1.call-done, u32[]{:T(128)S(6)} %multiply.19), kind=kOutput, calls=%fused_computation.13 | convolution fusion | flops 465567744 | bytes 114692 | tf_op jit(solution)/shard_map/dot_general | solution.py:116
  223.9 69.1 %fusion.3 = f32[8,2048]{1,0:T(8,128)S(1)} fusion(s32[2048]{0:T(1024)S(1)} %get-tuple-element.35, s32[2048]{0:T(1024)S(1)} %get-tuple-element.36, bf16[32,2,2048]{2,0,1:T(8,128)(2,1)} %all-reduce.5.cloned.1.call-done, u32[]{:T(128)S(6)} %multiply.19, u32[]{:T(128)S(6)} %convert.18), kind=kOutput, calls=%fused_computation.12 | convolution fusion | flops 465567744 | bytes 114696 | tf_op jit(solution)/shard_map/dot_general | solution.py:119
  293.0 69.3 %fusion.20 = bf16[8,1,2048]{2,0,1:T(8,128)(2,1)S(1)} fusion(f32[8,2048]{1,0:T(8,128)S(1)} %fusion.4, s32[2048]{0:T(1024)S(1)} %get-tuple-element.35, s32[2048]{0:T(1024)S(1)} %get-tuple-element.36, bf16[32,2,2048]{2,0,1:T(8,128)(2,1)} %all-reduce.5.cloned.1.call-done, u32[]{:T(128)S(6)} %multiply.19, u32[]{:T(128)S(6)} %convert.18), kind=kOutput, calls=%fused_computation.27 | convolution fusion | flops 465600512 | bytes 147464 | tf_op jit(solution)/shard_map/dot_general | solution.py:116
  362.4 69.4 %fusion.21 = bf16[8,1,2048]{2,0,1:T(8,128)(2,1)S(1)} fusion(f32[8,2048]{1,0:T(8,128)S(1)} %fusion.3, s32[2048]{0:T(1024)S(1)} %get-tuple-element.35, s32[2048]{0:T(1024)S(1)} %get-tuple-element.36, bf16[32,2,2048]{2,0,1:T(8,128)(2,1)} %all-reduce.5.cloned.1.call-done, u32[]{:T(128)S(6)} %multiply.19), kind=kOutput, calls=%fused_computation.28 | convolution fusion | flops 465600512 | bytes 147460 | tf_op jit(solution)/shard_map/dot_general | solution.py:119
  431.8 0.7 copy.24
  432.5 0.7 dynamic-slice.6
  433.2 53.1 %all-reduce.7.cloned.1.call-done = bf16[8,2,2048]{2,1,0:T(2,128)(2,1)} async-done(((bf16[8,2,2048]{2,1,0:T(2,128)(2,1)}), bf16[8,2,2048]{2,1,0:T(2,128)(2,1)}) %all-reduce.7.cloned.1.call-update) | async-done | bytes 65552
  486.2 2.0 dynamic-slice_convert_fusion
  (41 shorter events, 2.8 us)
Async XLA Ops:
  22.5 5.7 %copy-start = (f32[2,16384]{1,0:T(2,128)S(1)}, f32[2,16384]{1,0:T(2,128)}, u32[]{:S(2)}) copy-start(f32[2,16384]{1,0:T(2,128)} %param.5) | copy-start | bytes 393220
  30.9 8.9 %copy-start.1 = (bf16[1,1,64,256]{3,2,1,0:T(8,128)(2,1)S(1)}, bf16[1,1,64,256]{3,2,1,0:T(8,128)(2,1)}, u32[]{:S(2)}) copy-start(bf16[1,1,64,256]{3,2,1,0:T(8,128)(2,1)} %param.6) | copy-start | bytes 98308
  30.9 9.1 %copy-start.2 = (s32[1,1,8]{2,1,0:T(1,128)S(1)}, s32[1,1,8]{2,1,0:T(1,128)}, u32[]{:S(2)}) copy-start(s32[1,1,8]{2,1,0:T(1,128)} %param.7) | copy-start | bytes 100
  33.5 55.5 %all-to-all-start = ((bf16[2,32,8,2048]{3,1,0,2:T(8,128)(2,1)}), bf16[2,32,8,2048]{3,1,0,2:T(8,128)(2,1)}, u32[]{:S(2)}, u32[]{:S(2)}) async-start(bf16[2,32,8,2048]{3,1,0,2:T(8,128)(2,1)} %copy.20), calls=%async_computation | async-start | bytes 4194304 | tf_op jit(solution)/shard_map/all_to_all | solution.py:82
  39.8 115.4 %all-reduce.5.cloned.1.call-start = ((), (), s32[]{:S(2)}) async-start(), calls=%async_computation.1 | async-start | bytes 524288
  111.7 1.8 copy-start.4
  113.2 373.0 %all-reduce.7.cloned.1.call-start = ((), (), s32[]{:S(2)}) async-start(), calls=%async_computation.2 | async-start | bytes 131072
  362.4 70.1 %copy-start.3 = (u32[32]{0:T(128)S(1)}, u32[32]{0:T(128)}, u32[]{:S(2)}) copy-start(u32[32]{0:T(128)} %constant.110) | copy-start | bytes 388
Sparse Core Ops, SparseCore 0:
  113.3 41.8 all-reduce.4
  432.6 53.5 all-reduce.6
where the time goes:
time: 504 us; the launch traced here: 495 us
  matrix products  290 us (58%)
  waiting for transfers between devices  142 us (28%)
  local copies, waits for them, and re-layouts  36.1 us (7%)
  between operations  14.6 us (3%)
  starting transfers between devices  6.66 us (1%)
  other arithmetic  5.47 us (1%)
    unnamed x4, waiting for transfers between devices  93.5 us
    dot_general x1, matrix products, local(): jnp.dot(summed[:, 0], range_sin, precision=HIGHEST_MODE)  69.4 us
    dot_general x1, matrix products, local(): jnp.dot(summed[:, 1], range_sin, precision=HIGHEST_MODE)  69.3 us
    dot_general x1, matrix products, local(): jnp.dot(summed[:, 1], range_cos, precision=HIGHEST_MODE)  69.1 us
    dot_general x1, matrix products, local(): jnp.dot(summed[:, 0], range_cos, precision=HIGHEST_MODE)  68.7 us
    all_to_all x1, waiting for transfers between devices, local(): lax.all_to_all(arranged, 'pul', split_axis=2, concat_axis=1, tiled=True)  48.5 us
    gather x24, local copies, waits for them, and re-layouts  18.1 us
  transfers between devices with their start and end apart: 3, of which 3 were waited for; matrix products, arithmetic and copies ran while one was open for 0% of the time, Pallas kernels for 0%

commit v1 on v0

v1 whole, which is shorter than its diff:
```python
import functools
import math

import jax
import jax.numpy as jnp
import ml_dtypes
import numpy as np
from jax import lax
from jax.experimental import pallas as pl
from jax.experimental.pallas import tpu as pltpu
from jax.sharding import PartitionSpec as P

FACTOR = 128
BLOCK_ROWS = 32
BAND_PULSES = 64
IMAGE_COLS = 2048
CHUNK = 32

BF = jnp.bfloat16
F32 = jnp.float32


def rounded(values):
    return np.asarray(values, np.float32).astype(ml_dtypes.bfloat16)


def turns(top, bottom):
    angle = np.mod(top, bottom) * (2.0 * math.pi / bottom)
    return np.cos(angle), np.sin(angle)


def complex_matrix(cos, sin):
    return np.block([[cos, -sin], [sin, cos]])


def range_tables():
    at = np.arange(FACTOR)
    grid = at[:, None] * at[None, :]
    cos, sin = turns(-grid, FACTOR)
    table = rounded(complex_matrix(cos, sin))
    twist = np.stack(turns(-grid, FACTOR * FACTOR)).astype(np.float32)
    return table, twist


def image_tables():
    at = np.arange(FACTOR)
    grid = at[:, None] * at[None, :]
    cos, sin = turns(grid, FACTOR)
    table = rounded(complex_matrix(cos, sin))
    twist = np.stack(turns(grid, FACTOR * FACTOR)).astype(np.float32)
    count = IMAGE_COLS // FACTOR
    high = np.arange(count) + (FACTOR * FACTOR - IMAGE_COLS) // 2 // FACTOR
    cos, sin = turns(high[:, None] * at[None, :], FACTOR)
    both = complex_matrix(cos, sin).reshape(2, count, 2 * FACTOR)
    last = rounded(both.transpose(1, 0, 2).reshape(2 * count, 2 * FACTOR))
    return table, twist, last


def azimuth_tables(image_rows, group_pulses, groups):
    total = group_pulses * groups
    chunks = image_rows // CHUNK
    row = np.arange(image_rows) - image_rows // 2
    cos, sin = turns(np.arange(group_pulses)[:, None] * row[None, :], total)
    cos = rounded(cos / math.sqrt(total)).astype(np.float32).reshape(-1, chunks, CHUNK)
    sin = rounded(sin / math.sqrt(total)).astype(np.float32).reshape(-1, chunks, CHUNK)
    table = np.concatenate([cos, sin, -sin, cos, -sin, cos, -cos, -sin], axis=2)
    turn_cos, turn_sin = turns(np.arange(groups)[:, None] * group_pulses * row[None, :], total)
    turn = np.stack([turn_cos, turn_sin], axis=1).reshape(groups, 2, chunks, CHUNK)
    turn = np.where(np.abs(turn) < 1e-9, 0.0, turn)
    turn = np.tile(turn, (1, 1, 1, 4)).transpose(0, 2, 1, 3)
    return rounded(table.reshape(group_pulses, chunks * 8 * CHUNK)), turn.astype(np.float32)


HBM = pl.BlockSpec(memory_space=pltpu.HBM)
VMEM = pl.BlockSpec(memory_space=pltpu.VMEM)
UNROLL = dict(wide=16, first=4, second=4, out=16, mix=1, image=4)


def in_hbm(*arrays):
    return [pltpu.with_memory_space_constraint(jnp.asarray(a), pltpu.HBM) for a in arrays]


def fetch(pairs, sems):
    copies = [pltpu.make_async_copy(a, b, sems.at[n]) for n, (a, b) in enumerate(pairs)]
    for copy in copies:
        copy.start()
    return copies


def mixing_kernel(
    blocks, chunks, offsets_hbm, weights_hbm, table_hbm, turn_hbm, out_ref,
    offsets_ref, weights_ref, table_ref, turn_ref, first_ref, second_ref, total_ref, other_ref, sems,
):
    width = 4 * CHUNK
    chunk = pl.program_id(0)
    group = lax.axis_index("ang")
    columns = pl.ds(pl.multiple_of(chunk * 2 * width, 2 * width), 2 * width) if chunks > 1 else slice(None)
    copies = fetch(
        [
            (weights_hbm.at[0, 0], weights_ref),
            (table_hbm.at[:, columns], table_ref),
            (offsets_hbm, offsets_ref),
            (turn_hbm.at[group, chunk], turn_ref),
        ],
        sems,
    )
    total_ref[...] = jnp.zeros_like(total_ref)
    other_ref[...] = jnp.zeros_like(other_ref)
    copies[0].wait()
    copies[1].wait()
    weights = weights_ref[...]
    column = lax.broadcasted_iota(jnp.int32, weights.shape, 1) // BLOCK_ROWS

    def multiply(block, carry):
        own = jnp.where(column == block, weights.astype(F32), 0.0).astype(BF)
        product = jnp.dot(own, table_ref[...], preferred_element_type=F32)
        first_ref[block] = product[:, :width]
        second_ref[block] = product[:, width:]
        return carry

    lax.fori_loop(0, blocks, multiply, 0, unroll=blocks <= 8)
    copies[2].wait()
    copies[3].wait()

    def place(block, carry):
        window = pl.ds(offsets_ref[0, 0, block], BAND_PULSES)
        total_ref[window, :] += first_ref[block]
        other_ref[window, :] += second_ref[block]
        return carry

    lax.fori_loop(0, blocks, place, 0)
    turn = turn_ref[...]
    out_ref[...] = (total_ref[...] * turn[0:1] + other_ref[...] * turn[1:2]).astype(BF)


def mixing(offsets, weights, table, turn):
    group_pulses, width = weights.shape[3], 4 * CHUNK
    chunks, blocks = table.shape[1] // (2 * width), offsets.shape[2]
    return pl.pallas_call(
        functools.partial(mixing_kernel, blocks, chunks),
        grid=(chunks,),
        out_shape=jax.ShapeDtypeStruct((group_pulses, chunks * width), BF),
        in_specs=[HBM] * 4,
        out_specs=pl.BlockSpec((group_pulses, width), lambda c: (0, c)),
        scratch_shapes=[
            pltpu.SMEM(offsets.shape, jnp.int32),
            pltpu.VMEM(weights.shape[2:], BF),
            pltpu.VMEM((group_pulses, 2 * width), BF),
            pltpu.VMEM(turn.shape[2:], F32),
            pltpu.VMEM((blocks, BAND_PULSES, width), F32),
            pltpu.VMEM((blocks, BAND_PULSES, width), F32),
            pltpu.VMEM((group_pulses, width), F32),
            pltpu.VMEM((group_pulses, width), F32),
            pltpu.SemaphoreType.DMA((4,)),
        ],
        compiler_params=pltpu.CompilerParams(vmem_limit_bytes=24 * 2**20),
        name="mixing",
    )(*in_hbm(offsets, weights, table, turn))


def turn_by(wave, j, twist_ref):
    real = wave[:FACTOR, j * FACTOR : (j + 1) * FACTOR]
    imag = wave[FACTOR:, j * FACTOR : (j + 1) * FACTOR]
    cos, sin = twist_ref[0], twist_ref[1]
    return jnp.concatenate([(real * cos - imag * sin).astype(BF), (real * sin + imag * cos).astype(BF)], axis=1)


def times_transposed(left, right):
    return lax.dot_general(left, right, (((1,), (1,)), ((), ())), preferred_element_type=F32)


def range_kernel(
    rows, pulses_hbm, filter_hbm, table_hbm, twist_hbm, out_ref,
    pulses_ref, filter_ref, table_ref, twist_ref, wide_ref, turned_ref, spec_ref, sems,
):
    parts = 8
    length = FACTOR // parts
    pieces = [
        (pulses_hbm.at[:, :, pl.ds(h * length * FACTOR, length * FACTOR)], pulses_ref.at[h]) for h in range(parts)
    ]
    copies = fetch(
        pieces + [(table_hbm, table_ref), (twist_hbm, twist_ref), (filter_hbm, filter_ref)], sems
    )
    for h in range(parts):
        copies[h].wait()
        for m in range(length):
            for c in range(2):
                wide_ref[c, (h * length + m) * rows : (h * length + m + 1) * rows, :] = pulses_ref[
                    h, c, :, m * FACTOR : (m + 1) * FACTOR
                ].astype(F32)
    copies[parts].wait()
    copies[parts + 1].wait()
    pair = 2

    def first(s, carry):
        sides = [
            jnp.concatenate(
                [wide_ref[c, pl.ds(s * pair + j, FACTOR, stride=rows), :].astype(BF) for c in range(2)], axis=0
            )
            for j in range(pair)
        ]
        section = jnp.dot(table_ref[...], jnp.concatenate(sides, axis=1), preferred_element_type=F32)
        for j in range(pair):
            turned_ref[s, j * FACTOR : (j + 1) * FACTOR, :] = turn_by(section, j, twist_ref)
        return carry

    lax.fori_loop(0, rows // pair, first, 0, unroll=UNROLL["first"])
    copies[parts + 2].wait()
    filter_real = filter_ref[:, 0, :] * (1.0 / FACTOR)
    filter_imag = filter_ref[:, 1, :] * (1.0 / FACTOR)
    spec_view = spec_ref

    def second(s, carry):
        wave = times_transposed(table_ref[...], turned_ref[s])
        for j in range(pair):
            p = s * pair + j
            real = wave[:FACTOR, j * FACTOR : (j + 1) * FACTOR]
            imag = wave[FACTOR:, j * FACTOR : (j + 1) * FACTOR]
            spec_view[pl.ds(p, FACTOR, stride=2 * rows), :] = real * filter_real - imag * filter_imag
            spec_view[pl.ds(rows + p, FACTOR, stride=2 * rows), :] = real * filter_imag + imag * filter_real
        return carry

    lax.fori_loop(0, rows // pair, second, 0, unroll=UNROLL["second"])

    def narrow(k2, carry):
        begin = pl.multiple_of(k2 * 2 * rows, 2 * rows)
        out_ref[k2] = spec_ref[pl.ds(begin, 2 * rows), :].astype(BF)
        return carry

    lax.fori_loop(0, FACTOR, narrow, 0, unroll=UNROLL["out"])


def range_forward(pulses, matched_filter, table, twist):
    rows, parts = pulses.shape[1], 8
    filters = matched_filter.reshape(2, FACTOR, FACTOR).transpose(1, 0, 2)
    return pl.pallas_call(
        functools.partial(range_kernel, rows),
        out_shape=jax.ShapeDtypeStruct((FACTOR, 2 * rows, FACTOR), BF),
        in_specs=[HBM] * 4,
        out_specs=VMEM,
        scratch_shapes=[
            pltpu.VMEM((parts, 2, rows, FACTOR * FACTOR // parts), BF),
            pltpu.VMEM((FACTOR, 2, FACTOR), F32),
            pltpu.VMEM((2 * FACTOR, 2 * FACTOR), BF),
            pltpu.VMEM((2, FACTOR, FACTOR), F32),
            pltpu.VMEM((2, FACTOR * rows, FACTOR), F32),
            pltpu.VMEM((rows // 2, 2 * FACTOR, 2 * FACTOR), BF),
            pltpu.VMEM((FACTOR * 2 * rows, FACTOR), F32),
            pltpu.SemaphoreType.DMA((parts + 3,)),
        ],
        compiler_params=pltpu.CompilerParams(vmem_limit_bytes=32 * 2**20),
        cost_estimate=pl.CostEstimate(flops=10**10, bytes_accessed=2**22, transcendentals=0),
        name="range_forward",
    )(*in_hbm(pulses, filters, table, twist))


def image_kernel(rows, tiles, spec_ref, mix_ref, table_ref, twist_ref, last_ref, out_ref, mixed_ref):
    wide = 2 * CHUNK
    for t in range(tiles):
        mix = mix_ref[t].astype(F32)
        mix = jnp.concatenate([mix[:, :wide], mix[:, wide:]], axis=0).T.astype(BF)
        for k2 in range(t * (FACTOR // tiles), (t + 1) * (FACTOR // tiles)):
            mixed_ref[k2 * wide : (k2 + 1) * wide, :] = jnp.dot(mix, spec_ref[k2], preferred_element_type=F32)
    pair = 2

    def step(s, carry):
        sides = [
            jnp.concatenate(
                [
                    mixed_ref[pl.ds(c * CHUNK + s * pair + j, FACTOR, stride=wide), :].astype(BF)
                    for c in range(2)
                ],
                axis=0,
            )
            for j in range(pair)
        ]
        wave = jnp.dot(table_ref[...], jnp.concatenate(sides, axis=1), preferred_element_type=F32)
        turned = jnp.concatenate([turn_by(wave, j, twist_ref) for j in range(pair)], axis=0)
        window = times_transposed(last_ref[...], turned) * (1.0 / FACTOR)
        for j in range(pair):
            out_ref[s * pair + j] = window[:, j * FACTOR : (j + 1) * FACTOR].astype(BF)
        return carry

    lax.fori_loop(0, CHUNK // pair, step, 0, unroll=UNROLL["image"])


def image_part(spec, mix, table, twist, last):
    tiles, rows = mix.shape[0], mix.shape[1]
    chunks = mix.shape[2] // (4 * CHUNK)
    whole = lambda array: pl.BlockSpec(array.shape, lambda c: (0,) * array.ndim)
    high = last.shape[0]
    return pl.pallas_call(
        functools.partial(image_kernel, rows, tiles),
        grid=(chunks,),
        out_shape=jax.ShapeDtypeStruct((chunks * CHUNK, high, FACTOR), BF),
        in_specs=[
            whole(spec),
            pl.BlockSpec((tiles, rows, 4 * CHUNK), lambda c: (0, 0, c)),
            whole(table),
            whole(twist),
            whole(last),
        ],
        out_specs=pl.BlockSpec((CHUNK, high, FACTOR), lambda c: (c, 0, 0)),
        scratch_shapes=[pltpu.VMEM((FACTOR * 2 * CHUNK, FACTOR), F32)],
        compiler_params=pltpu.CompilerParams(vmem_limit_bytes=32 * 2**20),
        name="image_part",
    )(spec, mix, table, twist, last)


def local(pulses, matched_filter, interp_weights, offsets):
    pul_count, ang_count = lax.axis_size("pul"), lax.axis_size("ang")
    image_rows, rows = pul_count * ang_count, pulses.shape[1]
    azimuth, turn = azimuth_tables(image_rows, rows * pul_count, ang_count)
    mix = mixing(offsets, interp_weights, azimuth, turn)
    mix = lax.all_to_all(
        mix.reshape(pul_count, rows, mix.shape[1]), "pul", split_axis=0, concat_axis=0, tiled=True
    )
    spec = range_forward(pulses, matched_filter, *range_tables())
    part = image_part(spec, mix, *image_tables())
    parts = lax.all_to_all(part, ("ang", "pul"), split_axis=0, concat_axis=0, tiled=True)
    image = jnp.sum(parts.astype(F32), axis=0)
    return image.reshape(-1, 2, FACTOR).transpose(1, 0, 2).reshape(1, 2, IMAGE_COLS)


def solution(mesh):
    placed = (
        P(None, ("ang", "pul"), None),
        P(),
        P("ang", "pul", None, None),
        P("ang", "pul", None),
    )
    return jax.shard_map(
        local, mesh=mesh, in_specs=placed, out_specs=P(("ang", "pul"), None, None), check_vma=False
    )
```

time: 504 us -> 40 us (0.08); the launches traced: 495 us -> 39.7 us
  matrix products: 290 us -> 0 us
  waiting for transfers between devices: 142 us -> 0.01 us
  local copies, waits for them, and re-layouts: 36.1 us -> 0.02 us
  Pallas kernels: 0 us -> 16.4 us
  blocking collectives: 0 us -> 16.3 us
  between operations: 14.6 us -> 0.07 us
    dot_general x14 -> x0, matrix products: 290 us -> none  [the longest x1 69.4 us: local(): jnp.dot(summed[:, 0], range_sin, precision=HIGHEST_MODE)]
    unnamed x4 -> x0, waiting for transfers between devices: 93.5 us -> none
    all_to_all x1, waiting for transfers between devices: 48.5 us -> 0.01 us  [local(): lax.all_to_all(mix.reshape(pul_count, rows, mix.shape[1]), 'pul', split_a...]
    gather x24 -> x0, local copies, waits for them, and re-layouts: 18.1 us -> none
    pallas_call x0 -> x3, Pallas kernels: none -> 16.4 us  [the longest x1 9.82 us: range_forward(): pl.pallas_call(functools.partial(range_kernel, rows), out_shape=jax.Shape...]
    all_to_all x0 -> x1, blocking collectives: none -> 16.3 us  [local(): lax.all_to_all(part, ('ang', 'pul'), split_axis=0, concat_axis=0, tiled=T...]
  transfers between devices with their start and end apart: 3 -> 1, of which waited for: 3 -> 0; matrix products, arithmetic and copies ran while one was open for 0% -> 0% of each run, Pallas kernels for 0% -> 25%
where the time goes in v1:
time: 40 us; the launch traced here: 39.7 us
  Pallas kernels  16.4 us (41%)
  blocking collectives  16.3 us (41%)
  starting transfers between devices  6.34 us (16%)
  other arithmetic  0.65 us (2%)
    all_to_all x1, blocking collectives, local(): lax.all_to_all(part, ('ang', 'pul'), split_axis=0, concat_axis=0, tiled=T...  16.3 us
    pallas_call x1, Pallas kernels, range_forward(): pl.pallas_call(functools.partial(range_kernel, rows), out_shape=jax.Shape...  9.82 us
    all_to_all x1, starting transfers between devices, local(): lax.all_to_all(mix.reshape(pul_count, rows, mix.shape[1]), 'pul', split_a...  6.34 us
    pallas_call x1, Pallas kernels, image_part(): pl.pallas_call(functools.partial(image_kernel, rows, tiles), grid=(chunks...  4.6 us
    pallas_call x1, Pallas kernels, mixing(): pl.pallas_call(functools.partial(mixing_kernel, blocks, chunks), grid=(ch...  1.98 us
  transfers between devices with their start and end apart: 1, of which 0 were waited for; matrix products, arithmetic and copies ran while one was open for 0% of the time, Pallas kernels for 25%

profile of v1, /device:TPU:0, one launch (start us, length us, event | category | flops | bytes accessed | tf_op | source)
XLA Modules:
  0.0 39.7 jit_solution(9915747059365014136)
XLA Ops:
  0.0 2.0 %mixing.1 = bf16[256,128]{1,0:T(8,128)(2,1)} custom-call(s32[1,1,8]{2,1,0:T(1,128)} %offsets_hbm.1, bf16[1,1,64,256]{3,2,1,0:T(8,128)(2,1)} %weights_hbm.1, bf16[256,256]{1,0:T(8,128)(2,1)} %constant.16.clone.table_hbm, f32[4,1,2,128]{3,2,1,0:T(2,128)} %constant.17.clone.turn_hbm), custom_call_target="tpu_custom_call" | custom-call | tf_op jit(solution)/shard_map/mixing/pallas_call | solution.py:139
  2.0 6.3 %all-to-all-start = ((bf16[8,32,128]{2,1,0:T(8,128)(2,1)}), bf16[8,32,128]{2,1,0:T(8,128)(2,1)S(1)}, u32[]{:S(2)}, u32[]{:S(2)}) async-start(bf16[8,32,128]{2,1,0:T(8,128)(2,1)} %bitcast.2), calls=%async_computation | async-start | bytes 131072 | tf_op jit(solution)/shard_map/all_to_all | solution.py:315
  8.3 0.0 copy-start
  8.3 0.0 copy-start.1
  8.3 0.0 copy-start.2
  8.4 9.8 %range_forward.1.spec_ref = bf16[128,64,128]{2,1,0:T(8,128)(2,1)S(1)} custom-call(bf16[2,32,16384]{2,1,0:T(8,128)(2,1)} %pulses_hbm.1, f32[128,2,128]{2,1,0:T(2,128)} %bitcast.9, bf16[256,256]{1,0:T(8,128)(2,1)} %constant.18.clone.table_hbm, f32[2,128,128]{2,1,0:T(8,128)} %constant.19.clone.twist_hbm), custom_call_target="tpu_custom_call" | custom-call | flops 10000000000 | bytes 4194304 | tf_op jit(solution)/shard_map/range_forward/pallas_call | solution.py:236
  18.2 0.0 all-to-all-done.mix_ref
  18.2 0.0 copy-done
  18.2 0.0 copy-done.1
  18.2 0.0 copy-done.2
  18.2 4.6 %image_part.1 = bf16[32,32,128]{2,1,0:T(8,128)(2,1)S(1)} custom-call(bf16[128,64,128]{2,1,0:T(8,128)(2,1)S(1)} %range_forward.1.spec_ref, bf16[8,32,128]{2,1,0:T(8,128)(2,1)S(1)} %all-to-all-done.mix_ref, bf16[256,256]{1,0:T(8,128)(2,1)S(1)} %copy-done.1, f32[2,128,128]{2,1,0:T(8,128)S(1)} %copy-done, bf16[32,256]{1,0:T(8,128)(2,1)S(1)} %copy-done.2), custom_call_target="tpu_custom_call" | custom-call | tf_op jit(solution)/shard_map/image_part/pallas_call | solution.py:292
  22.8 16.3 %all_to_all.10 = bf16[32,32,128]{2,1,0:T(8,128)(2,1)S(1)} all-to-all(bf16[32,32,128]{2,1,0:T(8,128)(2,1)S(1)} %image_part.1), channel_id=1, replica_groups=mesh['ang'=4,'pul'=8] {'ang','pul'}, dimensions={0} | all-to-all | bytes 524288 | tf_op jit(solution)/shard_map/all_to_all | solution.py:320
  39.1 0.7 %convert_reduce_fusion = f32[32,128]{1,0:T(8,128)} fusion(bf16[32,32,128]{2,1,0:T(8,128)(2,1)S(1)} %all_to_all.10), kind=kLoop, calls=%fused_computation | loop fusion | flops 258048 | bytes 278528 | tf_op jit(solution)/shard_map/reduce_sum | solution.py:321
Async XLA Ops:
  2.0 16.2 %all-to-all-start = ((bf16[8,32,128]{2,1,0:T(8,128)(2,1)}), bf16[8,32,128]{2,1,0:T(8,128)(2,1)S(1)}, u32[]{:S(2)}, u32[]{:S(2)}) async-start(bf16[8,32,128]{2,1,0:T(8,128)(2,1)} %bitcast.2), calls=%async_computation | async-start | bytes 131072 | tf_op jit(solution)/shard_map/all_to_all | solution.py:315
  8.3 9.9 %copy-start = (f32[2,128,128]{2,1,0:T(8,128)S(1)}, f32[2,128,128]{2,1,0:T(8,128)}, u32[]{:S(2)}) copy-start(f32[2,128,128]{2,1,0:T(8,128)} %constant.21.clone.twist_ref) | copy-start | bytes 393220
  8.3 9.9 %copy-start.1 = (bf16[256,256]{1,0:T(8,128)(2,1)S(1)}, bf16[256,256]{1,0:T(8,128)(2,1)}, u32[]{:S(2)}) copy-start(bf16[256,256]{1,0:T(8,128)(2,1)} %constant.20.clone.table_ref) | copy-start | bytes 393220
  8.3 9.9 %copy-start.2 = (bf16[32,256]{1,0:T(8,128)(2,1)S(1)}, bf16[32,256]{1,0:T(8,128)(2,1)}, u32[]{:S(2)}) copy-start(bf16[32,256]{1,0:T(8,128)(2,1)} %constant.22.clone.last_ref) | copy-start | bytes 49156

commit v2 on v1

--- a/solution.py
+++ b/solution.py
@@ -73,7 +73,8 @@
 
 HBM = pl.BlockSpec(memory_space=pltpu.HBM)
 VMEM = pl.BlockSpec(memory_space=pltpu.VMEM)
-UNROLL = dict(wide=16, first=4, second=4, out=16, mix=1, image=4)
+PAD = 1
+UNROLL = dict(first=8, second=8, out=2, image=8)
 
 
 def in_hbm(*arrays):
@@ -185,7 +186,7 @@
         copies[h].wait()
         for m in range(length):
             for c in range(2):
-                wide_ref[c, (h * length + m) * rows : (h * length + m + 1) * rows, :] = pulses_ref[
+                wide_ref[c, pl.ds((h * length + m) * (rows + PAD), rows), :] = pulses_ref[
                     h, c, :, m * FACTOR : (m + 1) * FACTOR
                 ].astype(F32)
     copies[parts].wait()
@@ -195,7 +196,7 @@
     def first(s, carry):
         sides = [
             jnp.concatenate(
-                [wide_ref[c, pl.ds(s * pair + j, FACTOR, stride=rows), :].astype(BF) for c in range(2)], axis=0
+                [wide_ref[c, pl.ds(s * pair + j, FACTOR, stride=rows + PAD), :].astype(BF) for c in range(2)], axis=0
             )
             for j in range(pair)
         ]
@@ -216,18 +217,19 @@
             p = s * pair + j
             real = wave[:FACTOR, j * FACTOR : (j + 1) * FACTOR]
             imag = wave[FACTOR:, j * FACTOR : (j + 1) * FACTOR]
-            spec_view[pl.ds(p, FACTOR, stride=2 * rows), :] = real * filter_real - imag * filter_imag
-            spec_view[pl.ds(rows + p, FACTOR, stride=2 * rows), :] = real * filter_imag + imag * filter_real
+            spec_view[pl.ds(p, FACTOR, stride=2 * rows + PAD), :] = real * filter_real - imag * filter_imag
+            spec_view[pl.ds(rows + p, FACTOR, stride=2 * rows + PAD), :] = real * filter_imag + imag * filter_real
         return carry
 
     lax.fori_loop(0, rows // pair, second, 0, unroll=UNROLL["second"])
 
-    def narrow(k2, carry):
-        begin = pl.multiple_of(k2 * 2 * rows, 2 * rows)
-        out_ref[k2] = spec_ref[pl.ds(begin, 2 * rows), :].astype(BF)
-        return carry
-
-    lax.fori_loop(0, FACTOR, narrow, 0, unroll=UNROLL["out"])
+    def narrow(step, carry):
+        begin = pl.multiple_of(step * 8 * (2 * rows + PAD), 8)
+        for n in range(8):
+            out_ref[step * 8 + n] = spec_ref[pl.ds(begin + n * (2 * rows + PAD), 2 * rows), :].astype(BF)
+        return carry
+
+    lax.fori_loop(0, FACTOR // 8, narrow, 0, unroll=UNROLL["out"])
 
 
 def range_forward(pulses, matched_filter, table, twist):
@@ -243,9 +245,9 @@
             pltpu.VMEM((FACTOR, 2, FACTOR), F32),
             pltpu.VMEM((2 * FACTOR, 2 * FACTOR), BF),
             pltpu.VMEM((2, FACTOR, FACTOR), F32),
-            pltpu.VMEM((2, FACTOR * rows, FACTOR), F32),
+            pltpu.VMEM((2, FACTOR * (rows + PAD), FACTOR), F32),
             pltpu.VMEM((rows // 2, 2 * FACTOR, 2 * FACTOR), BF),
-            pltpu.VMEM((FACTOR * 2 * rows, FACTOR), F32),
+            pltpu.VMEM((FACTOR * (2 * rows + PAD), FACTOR), F32),
             pltpu.SemaphoreType.DMA((parts + 3,)),
         ],
         compiler_params=pltpu.CompilerParams(vmem_limit_bytes=32 * 2**20),
@@ -260,14 +262,14 @@
         mix = mix_ref[t].astype(F32)
         mix = jnp.concatenate([mix[:, :wide], mix[:, wide:]], axis=0).T.astype(BF)
         for k2 in range(t * (FACTOR // tiles), (t + 1) * (FACTOR // tiles)):
-            mixed_ref[k2 * wide : (k2 + 1) * wide, :] = jnp.dot(mix, spec_ref[k2], preferred_element_type=F32)
+            mixed_ref[pl.ds(k2 * (wide + PAD), wide), :] = jnp.dot(mix, spec_ref[k2], preferred_element_type=F32)
     pair = 2
 
     def step(s, carry):
         sides = [
             jnp.concatenate(
                 [
-                    mixed_ref[pl.ds(c * CHUNK + s * pair + j, FACTOR, stride=wide), :].astype(BF)
+                    mixed_ref[pl.ds(c * CHUNK + s * pair + j, FACTOR, stride=wide + PAD), :].astype(BF)
                     for c in range(2)
                 ],
                 axis=0,
@@ -301,7 +303,7 @@
             whole(last),
         ],
         out_specs=pl.BlockSpec((CHUNK, high, FACTOR), lambda c: (c, 0, 0)),
-        scratch_shapes=[pltpu.VMEM((FACTOR * 2 * CHUNK, FACTOR), F32)],
+        scratch_shapes=[pltpu.VMEM((FACTOR * (2 * CHUNK + PAD), FACTOR), F32)],
         compiler_params=pltpu.CompilerParams(vmem_limit_bytes=32 * 2**20),
         name="image_part",
     )(spec, mix, table, twist, last)

time: 40 us -> 32.4 us (0.81)
  Pallas kernels: 16.4 us -> 8.77 us
  waiting for transfers between devices: 0.01 us -> 1.62 us
  blocking collectives: 16.3 us -> 14.7 us
    pallas_call x1, Pallas kernels: 9.82 us -> 4.26 us  [range_forward(): pl.pallas_call(functools.partial(range_kernel, rows), out_shape=jax.Shape...]
    pallas_call x1, Pallas kernels: 4.6 us -> 2.54 us  [image_part(): pl.pallas_call(functools.partial(image_kernel, rows, tiles), grid=(chunks...]
    all_to_all x1, waiting for transfers between devices: 0.01 us -> 1.62 us  [local(): lax.all_to_all(mix.reshape(pul_count, rows, mix.shape[1]), 'pul', split_a...]
    all_to_all x1, blocking collectives: 16.3 us -> 14.7 us  [local(): lax.all_to_all(part, ('ang', 'pul'), split_axis=0, concat_axis=0, tiled=T...]
  transfers between devices with their start and end apart: 1 -> 1, of which waited for: 0 -> 1; matrix products, arithmetic and copies ran while one was open for 0% -> 0% of each run, Pallas kernels for 25% -> 13%
where the time goes in v2:
time: 32.4 us; the launch traced here: 32.1 us
  blocking collectives  14.7 us (45%)
  Pallas kernels  8.77 us (27%)
  starting transfers between devices  6.34 us (20%)
  waiting for transfers between devices  1.62 us (5%)
  other arithmetic  0.65 us (2%)
    all_to_all x1, blocking collectives, local(): lax.all_to_all(part, ('ang', 'pul'), split_axis=0, concat_axis=0, tiled=T...  14.7 us
    all_to_all x1, starting transfers between devices, local(): lax.all_to_all(mix.reshape(pul_count, rows, mix.shape[1]), 'pul', split_a...  6.34 us
    pallas_call x1, Pallas kernels, range_forward(): pl.pallas_call(functools.partial(range_kernel, rows), out_shape=jax.Shape...  4.26 us
    pallas_call x1, Pallas kernels, image_part(): pl.pallas_call(functools.partial(image_kernel, rows, tiles), grid=(chunks...  2.54 us
    pallas_call x1, Pallas kernels, mixing(): pl.pallas_call(functools.partial(mixing_kernel, blocks, chunks), grid=(ch...  1.98 us
    all_to_all x1, waiting for transfers between devices, local(): lax.all_to_all(mix.reshape(pul_count, rows, mix.shape[1]), 'pul', split_a...  1.62 us
    reduce_sum x1, other arithmetic, local(): image = jnp.sum(parts.astype(F32), axis=0)  0.65 us
  transfers between devices with their start and end apart: 1, of which 1 were waited for; matrix products, arithmetic and copies ran while one was open for 0% of the time, Pallas kernels for 13%

profile of v2, /device:TPU:0, one launch (start us, length us, event | category | flops | bytes accessed | tf_op | source)
XLA Modules:
  0.0 32.1 jit_solution(13024149804373096907)
XLA Ops:
  0.0 2.0 %mixing.1 = bf16[256,128]{1,0:T(8,128)(2,1)} custom-call(s32[1,1,8]{2,1,0:T(1,128)} %offsets_hbm.1, bf16[1,1,64,256]{3,2,1,0:T(8,128)(2,1)} %weights_hbm.1, bf16[256,256]{1,0:T(8,128)(2,1)} %constant.16.clone.table_hbm, f32[4,1,2,128]{3,2,1,0:T(2,128)} %constant.17.clone.turn_hbm), custom_call_target="tpu_custom_call" | custom-call | tf_op jit(solution)/shard_map/mixing/pallas_call | solution.py:140
  2.0 6.3 %all-to-all-start = ((bf16[8,32,128]{2,1,0:T(8,128)(2,1)}), bf16[8,32,128]{2,1,0:T(8,128)(2,1)S(1)}, u32[]{:S(2)}, u32[]{:S(2)}) async-start(bf16[8,32,128]{2,1,0:T(8,128)(2,1)} %bitcast.2), calls=%async_computation | async-start | bytes 131072 | tf_op jit(solution)/shard_map/all_to_all | solution.py:317
  8.3 0.0 copy-start
  8.3 0.0 copy-start.1
  8.3 0.0 copy-start.2
  8.4 4.3 %range_forward.1.spec_ref = bf16[128,64,128]{2,1,0:T(8,128)(2,1)S(1)} custom-call(bf16[2,32,16384]{2,1,0:T(8,128)(2,1)} %pulses_hbm.1, f32[128,2,128]{2,1,0:T(2,128)} %bitcast.9, bf16[256,256]{1,0:T(8,128)(2,1)} %constant.18.clone.table_hbm, f32[2,128,128]{2,1,0:T(8,128)} %constant.19.clone.twist_hbm), custom_call_target="tpu_custom_call" | custom-call | flops 10000000000 | bytes 4194304 | tf_op jit(solution)/shard_map/range_forward/pallas_call | solution.py:238
  12.6 1.6 %all-to-all-done.mix_ref = bf16[8,32,128]{2,1,0:T(8,128)(2,1)S(1)} async-done(((bf16[8,32,128]{2,1,0:T(8,128)(2,1)}), bf16[8,32,128]{2,1,0:T(8,128)(2,1)S(1)}, u32[]{:S(2)}, u32[]{:S(2)}) %all-to-all-start) | async-done | bytes 65568 | tf_op jit(solution)/shard_map/all_to_all | solution.py:317
  14.2 0.0 copy-done
  14.2 0.0 copy-done.1
  14.2 0.0 copy-done.2
  14.3 2.5 %image_part.1 = bf16[32,32,128]{2,1,0:T(8,128)(2,1)S(1)} custom-call(bf16[128,64,128]{2,1,0:T(8,128)(2,1)S(1)} %range_forward.1.spec_ref, bf16[8,32,128]{2,1,0:T(8,128)(2,1)S(1)} %all-to-all-done.mix_ref, bf16[256,256]{1,0:T(8,128)(2,1)S(1)} %copy-done.1, f32[2,128,128]{2,1,0:T(8,128)S(1)} %copy-done, bf16[32,256]{1,0:T(8,128)(2,1)S(1)} %copy-done.2), custom_call_target="tpu_custom_call" | custom-call | tf_op jit(solution)/shard_map/image_part/pallas_call | solution.py:294
  16.8 14.7 %all_to_all.10 = bf16[32,32,128]{2,1,0:T(8,128)(2,1)S(1)} all-to-all(bf16[32,32,128]{2,1,0:T(8,128)(2,1)S(1)} %image_part.1), channel_id=1, replica_groups=mesh['ang'=4,'pul'=8] {'ang','pul'}, dimensions={0} | all-to-all | bytes 524288 | tf_op jit(solution)/shard_map/all_to_all | solution.py:322
  31.4 0.7 %convert_reduce_fusion = f32[32,128]{1,0:T(8,128)} fusion(bf16[32,32,128]{2,1,0:T(8,128)(2,1)S(1)} %all_to_all.10), kind=kLoop, calls=%fused_computation | loop fusion | flops 258048 | bytes 278528 | tf_op jit(solution)/shard_map/reduce_sum | solution.py:323
Async XLA Ops:
  2.0 12.3 %all-to-all-start = ((bf16[8,32,128]{2,1,0:T(8,128)(2,1)}), bf16[8,32,128]{2,1,0:T(8,128)(2,1)S(1)}, u32[]{:S(2)}, u32[]{:S(2)}) async-start(bf16[8,32,128]{2,1,0:T(8,128)(2,1)} %bitcast.2), calls=%async_computation | async-start | bytes 131072 | tf_op jit(solution)/shard_map/all_to_all | solution.py:317
  8.3 5.9 %copy-start = (f32[2,128,128]{2,1,0:T(8,128)S(1)}, f32[2,128,128]{2,1,0:T(8,128)}, u32[]{:S(2)}) copy-start(f32[2,128,128]{2,1,0:T(8,128)} %constant.21.clone.twist_ref) | copy-start | bytes 393220
  8.3 5.9 %copy-start.1 = (bf16[256,256]{1,0:T(8,128)(2,1)S(1)}, bf16[256,256]{1,0:T(8,128)(2,1)}, u32[]{:S(2)}) copy-start(bf16[256,256]{1,0:T(8,128)(2,1)} %constant.20.clone.table_ref) | copy-start | bytes 393220
  8.3 5.9 %copy-start.2 = (bf16[32,256]{1,0:T(8,128)(2,1)S(1)}, bf16[32,256]{1,0:T(8,128)(2,1)}, u32[]{:S(2)}) copy-start(bf16[32,256]{1,0:T(8,128)(2,1)} %constant.22.clone.last_ref) | copy-start | bytes 49156

commit v3 on v2

--- a/solution.py
+++ b/solution.py
@@ -63,18 +63,20 @@
     cos, sin = turns(np.arange(group_pulses)[:, None] * row[None, :], total)
     cos = rounded(cos / math.sqrt(total)).astype(np.float32).reshape(-1, chunks, CHUNK)
     sin = rounded(sin / math.sqrt(total)).astype(np.float32).reshape(-1, chunks, CHUNK)
-    table = np.concatenate([cos, sin, -sin, cos, -sin, cos, -cos, -sin], axis=2)
+    table = np.concatenate([cos, sin, -sin, cos], axis=2)
     turn_cos, turn_sin = turns(np.arange(groups)[:, None] * group_pulses * row[None, :], total)
     turn = np.stack([turn_cos, turn_sin], axis=1).reshape(groups, 2, chunks, CHUNK)
     turn = np.where(np.abs(turn) < 1e-9, 0.0, turn)
-    turn = np.tile(turn, (1, 1, 1, 4)).transpose(0, 2, 1, 3)
-    return rounded(table.reshape(group_pulses, chunks * 8 * CHUNK)), turn.astype(np.float32)
+    turn = np.tile(turn, (1, 1, 1, 4))
+    turn[:, 1, :, 2 * CHUNK :] *= -1.0
+    turn = turn.transpose(0, 2, 1, 3)
+    return rounded(table.reshape(group_pulses, chunks * 4 * CHUNK)), turn.astype(np.float32)
 
 
 HBM = pl.BlockSpec(memory_space=pltpu.HBM)
 VMEM = pl.BlockSpec(memory_space=pltpu.VMEM)
 PAD = 1
-UNROLL = dict(first=8, second=8, out=2, image=8)
+UNROLL = dict(first=8, second=8, out=2, image=16)
 
 
 def in_hbm(*arrays):
@@ -90,67 +92,66 @@
 
 def mixing_kernel(
     blocks, chunks, offsets_hbm, weights_hbm, table_hbm, turn_hbm, out_ref,
-    offsets_ref, weights_ref, table_ref, turn_ref, first_ref, second_ref, total_ref, other_ref, sems,
+    offsets_ref, weights_ref, table_ref, turn_ref, product_ref, total_ref, sems,
 ):
     width = 4 * CHUNK
-    chunk = pl.program_id(0)
-    group = lax.axis_index("ang")
-    columns = pl.ds(pl.multiple_of(chunk * 2 * width, 2 * width), 2 * width) if chunks > 1 else slice(None)
     copies = fetch(
         [
             (weights_hbm.at[0, 0], weights_ref),
-            (table_hbm.at[:, columns], table_ref),
+            (table_hbm, table_ref),
             (offsets_hbm, offsets_ref),
-            (turn_hbm.at[group, chunk], turn_ref),
+            (turn_hbm.at[lax.axis_index("ang")], turn_ref),
         ],
         sems,
     )
-    total_ref[...] = jnp.zeros_like(total_ref)
-    other_ref[...] = jnp.zeros_like(other_ref)
-    copies[0].wait()
-    copies[1].wait()
+    for copy in copies:
+        copy.wait()
     weights = weights_ref[...]
     column = lax.broadcasted_iota(jnp.int32, weights.shape, 1) // BLOCK_ROWS
 
-    def multiply(block, carry):
-        own = jnp.where(column == block, weights.astype(F32), 0.0).astype(BF)
-        product = jnp.dot(own, table_ref[...], preferred_element_type=F32)
-        first_ref[block] = product[:, :width]
-        second_ref[block] = product[:, width:]
-        return carry
-
-    lax.fori_loop(0, blocks, multiply, 0, unroll=blocks <= 8)
-    copies[2].wait()
-    copies[3].wait()
-
-    def place(block, carry):
-        window = pl.ds(offsets_ref[0, 0, block], BAND_PULSES)
-        total_ref[window, :] += first_ref[block]
-        other_ref[window, :] += second_ref[block]
-        return carry
-
-    lax.fori_loop(0, blocks, place, 0)
-    turn = turn_ref[...]
-    out_ref[...] = (total_ref[...] * turn[0:1] + other_ref[...] * turn[1:2]).astype(BF)
+    def make(chunk):
+        columns = pl.ds(pl.multiple_of(chunk * width, width), width)
+        total_ref[...] = jnp.zeros_like(total_ref)
+        table = table_ref[:, columns]
+
+        def multiply(block, carry):
+            own = jnp.where(column == block, weights.astype(F32), 0.0).astype(BF)
+            product_ref[block] = jnp.dot(own, table, preferred_element_type=F32)
+            return carry
+
+        lax.fori_loop(0, blocks, multiply, 0, unroll=blocks <= 8)
+
+        def place(block, carry):
+            window = pl.ds(offsets_ref[0, 0, block], BAND_PULSES)
+            total_ref[window, :] += product_ref[block]
+            return carry
+
+        lax.fori_loop(0, blocks, place, 0)
+        turn = turn_ref[chunk]
+        total = total_ref[...]
+        other = pltpu.roll(total, width // 2, 1)
+        out_ref[:, columns] = (total * turn[0:1] + other * turn[1:2]).astype(BF)
+
+    if chunks == 1:
+        make(0)
+    else:
+        pl.loop(0, chunks)(make)
 
 
 def mixing(offsets, weights, table, turn):
     group_pulses, width = weights.shape[3], 4 * CHUNK
-    chunks, blocks = table.shape[1] // (2 * width), offsets.shape[2]
+    chunks, blocks = table.shape[1] // width, offsets.shape[2]
     return pl.pallas_call(
         functools.partial(mixing_kernel, blocks, chunks),
-        grid=(chunks,),
         out_shape=jax.ShapeDtypeStruct((group_pulses, chunks * width), BF),
         in_specs=[HBM] * 4,
-        out_specs=pl.BlockSpec((group_pulses, width), lambda c: (0, c)),
+        out_specs=VMEM,
         scratch_shapes=[
             pltpu.SMEM(offsets.shape, jnp.int32),
             pltpu.VMEM(weights.shape[2:], BF),
-            pltpu.VMEM((group_pulses, 2 * width), BF),
-            pltpu.VMEM(turn.shape[2:], F32),
+            pltpu.VMEM(table.shape, BF),
+            pltpu.VMEM(turn.shape[1:], F32),
             pltpu.VMEM((blocks, BAND_PULSES, width), F32),
-            pltpu.VMEM((blocks, BAND_PULSES, width), F32),
-            pltpu.VMEM((group_pulses, width), F32),
             pltpu.VMEM((group_pulses, width), F32),
             pltpu.SemaphoreType.DMA((4,)),
         ],
@@ -209,7 +210,6 @@
     copies[parts + 2].wait()
     filter_real = filter_ref[:, 0, :] * (1.0 / FACTOR)
     filter_imag = filter_ref[:, 1, :] * (1.0 / FACTOR)
-    spec_view = spec_ref
 
     def second(s, carry):
         wave = times_transposed(table_ref[...], turned_ref[s])
@@ -217,8 +217,8 @@
             p = s * pair + j
             real = wave[:FACTOR, j * FACTOR : (j + 1) * FACTOR]
             imag = wave[FACTOR:, j * FACTOR : (j + 1) * FACTOR]
-            spec_view[pl.ds(p, FACTOR, stride=2 * rows + PAD), :] = real * filter_real - imag * filter_imag
-            spec_view[pl.ds(rows + p, FACTOR, stride=2 * rows + PAD), :] = real * filter_imag + imag * filter_real
+            spec_ref[pl.ds(p, FACTOR, stride=2 * rows + PAD), :] = real * filter_real - imag * filter_imag
+            spec_ref[pl.ds(rows + p, FACTOR, stride=2 * rows + PAD), :] = real * filter_imag + imag * filter_real
         return carry
 
     lax.fori_loop(0, rows // pair, second, 0, unroll=UNROLL["second"])
@@ -256,7 +256,7 @@
     )(*in_hbm(pulses, filters, table, twist))
 
 
-def image_kernel(rows, tiles, spec_ref, mix_ref, table_ref, twist_ref, last_ref, out_ref, mixed_ref):
+def image_kernel(rows, tiles, spec_ref, mix_ref, table_ref, twist_ref, last_ref, keep_ref, give_ref, mixed_ref):
     wide = 2 * CHUNK
     for t in range(tiles):
         mix = mix_ref[t].astype(F32)
@@ -264,6 +264,15 @@
         for k2 in range(t * (FACTOR // tiles), (t + 1) * (FACTOR // tiles)):
             mixed_ref[pl.ds(k2 * (wide + PAD), wide), :] = jnp.dot(mix, spec_ref[k2], preferred_element_type=F32)
     pair = 2
+    half = last_ref.shape[0] // 2
+    core = lax.rem(lax.axis_index("pul"), 2)
+    last = jnp.concatenate(
+        [
+            last_ref[pl.ds(pl.multiple_of(core * half, half), half), :],
+            last_ref[pl.ds(pl.multiple_of((1 - core) * half, half), half), :],
+        ],
+        axis=0,
+    )
 
     def step(s, carry):
         sides = [
@@ -278,9 +287,10 @@
         ]
         wave = jnp.dot(table_ref[...], jnp.concatenate(sides, axis=1), preferred_element_type=F32)
         turned = jnp.concatenate([turn_by(wave, j, twist_ref) for j in range(pair)], axis=0)
-        window = times_transposed(last_ref[...], turned) * (1.0 / FACTOR)
+        window = times_transposed(last, turned) * (1.0 / FACTOR)
         for j in range(pair):
-            out_ref[s * pair + j] = window[:, j * FACTOR : (j + 1) * FACTOR].astype(BF)
+            keep_ref[s * pair + j] = window[:half, j * FACTOR : (j + 1) * FACTOR].astype(BF)
+            give_ref[s * pair + j] = window[half:, j * FACTOR : (j + 1) * FACTOR].astype(BF)
         return carry
 
     lax.fori_loop(0, CHUNK // pair, step, 0, unroll=UNROLL["image"])
@@ -294,7 +304,7 @@
     return pl.pallas_call(
         functools.partial(image_kernel, rows, tiles),
         grid=(chunks,),
-        out_shape=jax.ShapeDtypeStruct((chunks * CHUNK, high, FACTOR), BF),
+        out_shape=[jax.ShapeDtypeStruct((chunks * CHUNK, high // 2, FACTOR), BF)] * 2,
         in_specs=[
             whole(spec),
             pl.BlockSpec((tiles, rows, 4 * CHUNK), lambda c: (0, 0, c)),
@@ -302,7 +312,7 @@
             whole(twist),
             whole(last),
         ],
-        out_specs=pl.BlockSpec((CHUNK, high, FACTOR), lambda c: (c, 0, 0)),
+        out_specs=[pl.BlockSpec((CHUNK, high // 2, FACTOR), lambda c: (c, 0, 0))] * 2,
         scratch_shapes=[pltpu.VMEM((FACTOR * (2 * CHUNK + PAD), FACTOR), F32)],
         compiler_params=pltpu.CompilerParams(vmem_limit_bytes=32 * 2**20),
         name="image_part",
@@ -318,9 +328,11 @@
         mix.reshape(pul_count, rows, mix.shape[1]), "pul", split_axis=0, concat_axis=0, tiled=True
     )
     spec = range_forward(pulses, matched_filter, *range_tables())
-    part = image_part(spec, mix, *image_tables())
+    keep, give = image_part(spec, mix, *image_tables())
+    got = lax.ppermute(give, "pul", [(i, i ^ 1) for i in range(pul_count)])
+    part = (keep.astype(F32) + got.astype(F32)).astype(BF)
     parts = lax.all_to_all(part, ("ang", "pul"), split_axis=0, concat_axis=0, tiled=True)
-    image = jnp.sum(parts.astype(F32), axis=0)
+    image = jnp.sum(parts.reshape(image_rows // 2, -1, FACTOR).astype(F32), axis=0)
     return image.reshape(-1, 2, FACTOR).transpose(1, 0, 2).reshape(1, 2, IMAGE_COLS)
 
 

time: 32.4 us -> 31.2 us (0.963)
  blocking collectives: 14.7 us -> 12.4 us
  waiting for transfers between devices: 1.62 us -> 2.95 us
  Pallas kernels: 8.77 us -> 8.36 us
    all_to_all x1, blocking collectives: 14.7 us -> 12.4 us  [local(): lax.all_to_all(part, ('ang', 'pul'), split_axis=0, concat_axis=0, tiled=T...]
    ppermute x0 -> x1, waiting for transfers between devices: none -> 1.33 us  [local(): got = lax.ppermute(give, 'pul', [(i, i ^ 1) for i in range(pul_count)])]
    pallas_call x1, Pallas kernels: 2.54 us -> 2.2 us  [image_part(): pl.pallas_call(functools.partial(image_kernel, rows, tiles), grid=(chunks...]
  transfers between devices with their start and end apart: 1 -> 2, of which waited for: 1 -> 2; matrix products, arithmetic and copies ran while one was open for 0% -> 0% of each run, Pallas kernels for 13% -> 14%
where the time goes in v3:
time: 31.2 us; the launch traced here: 30.9 us
  blocking collectives  12.4 us (40%)
  Pallas kernels  8.36 us (27%)
  starting transfers between devices  6.41 us (21%)
  waiting for transfers between devices  2.95 us (9%)
  other arithmetic  0.66 us (2%)
    all_to_all x1, blocking collectives, local(): lax.all_to_all(part, ('ang', 'pul'), split_axis=0, concat_axis=0, tiled=T...  12.4 us
    all_to_all x1, starting transfers between devices, local(): lax.all_to_all(mix.reshape(pul_count, rows, mix.shape[1]), 'pul', split_a...  6.34 us
    pallas_call x1, Pallas kernels, range_forward(): pl.pallas_call(functools.partial(range_kernel, rows), out_shape=jax.Shape...  4.26 us
    pallas_call x1, Pallas kernels, image_part(): pl.pallas_call(functools.partial(image_kernel, rows, tiles), grid=(chunks...  2.2 us
    pallas_call x1, Pallas kernels, mixing(): pl.pallas_call(functools.partial(mixing_kernel, blocks, chunks), out_shap...  1.91 us
    all_to_all x1, waiting for transfers between devices, local(): lax.all_to_all(mix.reshape(pul_count, rows, mix.shape[1]), 'pul', split_a...  1.62 us
    ppermute x1, waiting for transfers between devices, local(): got = lax.ppermute(give, 'pul', [(i, i ^ 1) for i in range(pul_count)])  1.33 us
    reduce_sum x1, other arithmetic, local(): jnp.sum(parts.reshape(image_rows // 2, -1, FACTOR).astype(F32), axis=0)  0.63 us
  transfers between devices with their start and end apart: 2, of which 2 were waited for; matrix products, arithmetic and copies ran while one was open for 0% of the time, Pallas kernels for 14%

profile of v3, /device:TPU:0, one launch (start us, length us, event | category | flops | bytes accessed | tf_op | source)
XLA Modules:
  0.0 30.9 jit_solution(5250318912607448650)
XLA Ops:
  0.0 1.9 %mixing.1 = bf16[256,128]{1,0:T(8,128)(2,1)} custom-call(s32[1,1,8]{2,1,0:T(1,128)} %offsets_hbm.1, bf16[1,1,64,256]{3,2,1,0:T(8,128)(2,1)} %weights_hbm.1, bf16[256,128]{1,0:T(8,128)(2,1)} %constant.16.clone.table_hbm, f32[4,1,2,128]{3,2,1,0:T(2,128)} %constant.17.clone.turn_hbm), custom_call_target="tpu_custom_call" | custom-call | tf_op jit(solution)/shard_map/mixing/pallas_call | solution.py:144
  1.9 6.3 %all-to-all-start = ((bf16[8,32,128]{2,1,0:T(8,128)(2,1)}), bf16[8,32,128]{2,1,0:T(8,128)(2,1)S(1)}, u32[]{:S(2)}, u32[]{:S(2)}) async-start(bf16[8,32,128]{2,1,0:T(8,128)(2,1)} %bitcast.2), calls=%async_computation | async-start | bytes 131072 | tf_op jit(solution)/shard_map/all_to_all | solution.py:327
  8.3 0.0 copy-start
  8.3 0.0 copy-start.1
  8.3 0.0 copy-start.2
  8.3 4.3 %range_forward.1.spec_ref = bf16[128,64,128]{2,1,0:T(8,128)(2,1)S(1)} custom-call(bf16[2,32,16384]{2,1,0:T(8,128)(2,1)} %pulses_hbm.1, f32[128,2,128]{2,1,0:T(2,128)} %bitcast.14, bf16[256,256]{1,0:T(8,128)(2,1)} %constant.18.clone.table_hbm, f32[2,128,128]{2,1,0:T(8,128)} %constant.19.clone.twist_hbm), custom_call_target="tpu_custom_call" | custom-call | flops 10000000000 | bytes 4194304 | tf_op jit(solution)/shard_map/range_forward/pallas_call | solution.py:238
  12.6 1.6 %all-to-all-done.mix_ref = bf16[8,32,128]{2,1,0:T(8,128)(2,1)S(1)} async-done(((bf16[8,32,128]{2,1,0:T(8,128)(2,1)}), bf16[8,32,128]{2,1,0:T(8,128)(2,1)S(1)}, u32[]{:S(2)}, u32[]{:S(2)}) %all-to-all-start) | async-done | bytes 65568 | tf_op jit(solution)/shard_map/all_to_all | solution.py:327
  14.2 0.0 copy-done
  14.2 0.0 copy-done.1
  14.2 0.0 copy-done.2
  14.2 2.2 %image_part.1 = (bf16[32,16,128]{2,1,0:T(8,128)(2,1)S(1)}, bf16[32,16,128]{2,1,0:T(8,128)(2,1)S(1)}) custom-call(bf16[128,64,128]{2,1,0:T(8,128)(2,1)S(1)} %range_forward.1.spec_ref, bf16[8,32,128]{2,1,0:T(8,128)(2,1)S(1)} %all-to-all-done.mix_ref, bf16[256,256]{1,0:T(8,128)(2,1)S(1)} %copy-done.1, f32[2,128,128]{2,1,0:T(8,128)S(1)} %copy-done, ...), custom_call_target="tpu_custom_call" | custom-call | tf_op jit(solution)/shard_map/image_part/pallas_call | solution.py:304
  16.4 0.1 collective-permute-start
  16.5 1.3 %collective-permute-done = bf16[32,16,128]{2,1,0:T(8,128)(2,1)S(1)} collective-permute-done((bf16[32,16,128]{2,1,0:T(8,128)(2,1)S(1)}, bf16[32,16,128]{2,1,0:T(8,128)(2,1)S(1)}, u32[]{:S(2)}, u32[]{:S(2)}) %collective-permute-start) | collective-permute-done | bytes 131104 | tf_op jit(solution)/shard_map/ppermute | solution.py:332
  17.8 12.4 %all_to_all.10 = bf16[32,16,128]{2,1,0:T(8,128)(2,1)S(1)} all-to-all(bf16[32,16,128]{2,1,0:T(8,128)(2,1)S(1)} %add_convert_fusion), channel_id=1, replica_groups=mesh['ang'=4,'pul'=8] {'ang','pul'}, dimensions={0} | all-to-all | bytes 262144 | tf_op jit(solution)/shard_map/all_to_all | solution.py:334
  30.3 0.6 %convert_reduce_fusion = f32[32,128]{1,0:T(8,128)} fusion(bf16[16,32,128]{2,1,0:T(8,128)(2,1)S(1)} %bitcast.13), kind=kLoop, calls=%fused_computation | loop fusion | flops 126976 | bytes 147456 | tf_op jit(solution)/shard_map/reduce_sum | solution.py:335
  (1 shorter events, 0.0 us)
Async XLA Ops:
  1.9 12.3 %all-to-all-start = ((bf16[8,32,128]{2,1,0:T(8,128)(2,1)}), bf16[8,32,128]{2,1,0:T(8,128)(2,1)S(1)}, u32[]{:S(2)}, u32[]{:S(2)}) async-start(bf16[8,32,128]{2,1,0:T(8,128)(2,1)} %bitcast.2), calls=%async_computation | async-start | bytes 131072 | tf_op jit(solution)/shard_map/all_to_all | solution.py:327
  8.3 5.9 %copy-start = (f32[2,128,128]{2,1,0:T(8,128)S(1)}, f32[2,128,128]{2,1,0:T(8,128)}, u32[]{:S(2)}) copy-start(f32[2,128,128]{2,1,0:T(8,128)} %constant.21.clone.twist_ref) | copy-start | bytes 393220
  8.3 5.9 %copy-start.1 = (bf16[256,256]{1,0:T(8,128)(2,1)S(1)}, bf16[256,256]{1,0:T(8,128)(2,1)}, u32[]{:S(2)}) copy-start(bf16[256,256]{1,0:T(8,128)(2,1)} %constant.20.clone.table_ref) | copy-start | bytes 393220
  8.3 5.9 %copy-start.2 = (bf16[32,256]{1,0:T(8,128)(2,1)S(1)}, bf16[32,256]{1,0:T(8,128)(2,1)}, u32[]{:S(2)}) copy-start(bf16[32,256]{1,0:T(8,128)(2,1)} %constant.22.clone.last_ref) | copy-start | bytes 49156
  16.4 1.4 %collective-permute-start = (bf16[32,16,128]{2,1,0:T(8,128)(2,1)S(1)}, bf16[32,16,128]{2,1,0:T(8,128)(2,1)S(1)}, u32[]{:S(2)}, u32[]{:S(2)}) collective-permute-start(bf16[32,16,128]{2,1,0:T(8,128)(2,1)S(1)} %get-tuple-element.8), channel_id=1, source_target_pairs={{0,1},{1,0},{2,3},{3,2},{4,5},{5,4},{6,7},{7,6},{8,9},{9,8},{10,11... | collective-permute-start | bytes 393224 | tf_op jit(solution)/shard_map/ppermute | solution.py:332

commit v4 on v3

--- a/solution.py
+++ b/solution.py
@@ -76,7 +76,7 @@
 HBM = pl.BlockSpec(memory_space=pltpu.HBM)
 VMEM = pl.BlockSpec(memory_space=pltpu.VMEM)
 PAD = 1
-UNROLL = dict(first=8, second=8, out=2, image=16)
+UNROLL = dict(range=16, out=2, image=16)
 
 
 def in_hbm(*arrays):
@@ -173,7 +173,7 @@
 
 def range_kernel(
     rows, pulses_hbm, filter_hbm, table_hbm, twist_hbm, out_ref,
-    pulses_ref, filter_ref, table_ref, twist_ref, wide_ref, turned_ref, spec_ref, sems,
+    pulses_ref, filter_ref, table_ref, twist_ref, wide_ref, spec_ref, sems,
 ):
     parts = 8
     length = FACTOR // parts
@@ -194,7 +194,11 @@
     copies[parts + 1].wait()
     pair = 2
 
-    def first(s, carry):
+    copies[parts + 2].wait()
+    filter_real = filter_ref[:, 0, :] * (1.0 / FACTOR)
+    filter_imag = filter_ref[:, 1, :] * (1.0 / FACTOR)
+
+    def both(s, carry):
         sides = [
             jnp.concatenate(
                 [wide_ref[c, pl.ds(s * pair + j, FACTOR, stride=rows + PAD), :].astype(BF) for c in range(2)], axis=0
@@ -202,17 +206,8 @@
             for j in range(pair)
         ]
         section = jnp.dot(table_ref[...], jnp.concatenate(sides, axis=1), preferred_element_type=F32)
-        for j in range(pair):
-            turned_ref[s, j * FACTOR : (j + 1) * FACTOR, :] = turn_by(section, j, twist_ref)
-        return carry
-
-    lax.fori_loop(0, rows // pair, first, 0, unroll=UNROLL["first"])
-    copies[parts + 2].wait()
-    filter_real = filter_ref[:, 0, :] * (1.0 / FACTOR)
-    filter_imag = filter_ref[:, 1, :] * (1.0 / FACTOR)
-
-    def second(s, carry):
-        wave = times_transposed(table_ref[...], turned_ref[s])
+        turned = jnp.concatenate([turn_by(section, j, twist_ref) for j in range(pair)], axis=0)
+        wave = times_transposed(table_ref[...], turned)
         for j in range(pair):
             p = s * pair + j
             real = wave[:FACTOR, j * FACTOR : (j + 1) * FACTOR]
@@ -221,7 +216,7 @@
             spec_ref[pl.ds(rows + p, FACTOR, stride=2 * rows + PAD), :] = real * filter_imag + imag * filter_real
         return carry
 
-    lax.fori_loop(0, rows // pair, second, 0, unroll=UNROLL["second"])
+    lax.fori_loop(0, rows // pair, both, 0, unroll=UNROLL["range"])
 
     def narrow(step, carry):
         begin = pl.multiple_of(step * 8 * (2 * rows + PAD), 8)
@@ -246,7 +241,6 @@
             pltpu.VMEM((2 * FACTOR, 2 * FACTOR), BF),
             pltpu.VMEM((2, FACTOR, FACTOR), F32),
             pltpu.VMEM((2, FACTOR * (rows + PAD), FACTOR), F32),
-            pltpu.VMEM((rows // 2, 2 * FACTOR, 2 * FACTOR), BF),
             pltpu.VMEM((FACTOR * (2 * rows + PAD), FACTOR), F32),
             pltpu.SemaphoreType.DMA((parts + 3,)),
         ],

time: 31.2 us -> 30.8 us (0.987)
  waiting for transfers between devices: 2.95 us -> 3.38 us
  Pallas kernels: 8.36 us -> 7.94 us
  blocking collectives: 12.4 us -> 12 us
    all_to_all x1, waiting for transfers between devices: 1.62 us -> 2.05 us  [local(): lax.all_to_all(mix.reshape(pul_count, rows, mix.shape[1]), 'pul', split_a...]
    pallas_call x1, Pallas kernels: 4.26 us -> 3.83 us  [range_forward(): pl.pallas_call(functools.partial(range_kernel, rows), out_shape=jax.Shape...]
    all_to_all x1, blocking collectives: 12.4 us -> 12 us  [local(): lax.all_to_all(part, ('ang', 'pul'), split_axis=0, concat_axis=0, tiled=T...]
  transfers between devices with their start and end apart: 2 -> 2, of which waited for: 2 -> 2; matrix products, arithmetic and copies ran while one was open for 0% -> 0% of each run, Pallas kernels for 14% -> 13%
where the time goes in v4:
time: 30.8 us; the launch traced here: 30.5 us
  blocking collectives  12 us (39%)
  Pallas kernels  7.94 us (26%)
  starting transfers between devices  6.41 us (21%)
  waiting for transfers between devices  3.38 us (11%)
  other arithmetic  0.66 us (2%)
    all_to_all x1, blocking collectives, local(): lax.all_to_all(part, ('ang', 'pul'), split_axis=0, concat_axis=0, tiled=T...  12 us
    all_to_all x1, starting transfers between devices, local(): lax.all_to_all(mix.reshape(pul_count, rows, mix.shape[1]), 'pul', split_a...  6.34 us
    pallas_call x1, Pallas kernels, range_forward(): pl.pallas_call(functools.partial(range_kernel, rows), out_shape=jax.Shape...  3.83 us
    pallas_call x1, Pallas kernels, image_part(): pl.pallas_call(functools.partial(image_kernel, rows, tiles), grid=(chunks...  2.21 us
    all_to_all x1, waiting for transfers between devices, local(): lax.all_to_all(mix.reshape(pul_count, rows, mix.shape[1]), 'pul', split_a...  2.05 us
    pallas_call x1, Pallas kernels, mixing(): pl.pallas_call(functools.partial(mixing_kernel, blocks, chunks), out_shap...  1.91 us
    ppermute x1, waiting for transfers between devices, local(): got = lax.ppermute(give, 'pul', [(i, i ^ 1) for i in range(pul_count)])  1.33 us
    reduce_sum x1, other arithmetic, local(): jnp.sum(parts.reshape(image_rows // 2, -1, FACTOR).astype(F32), axis=0)  0.63 us
  transfers between devices with their start and end apart: 2, of which 2 were waited for; matrix products, arithmetic and copies ran while one was open for 0% of the time, Pallas kernels for 13%

profile of v4, /device:TPU:0, one launch (start us, length us, event | category | flops | bytes accessed | tf_op | source)
XLA Modules:
  0.0 30.5 jit_solution(6745388992564593710)
XLA Ops:
  0.0 1.9 %mixing.1 = bf16[256,128]{1,0:T(8,128)(2,1)} custom-call(s32[1,1,8]{2,1,0:T(1,128)} %offsets_hbm.1, bf16[1,1,64,256]{3,2,1,0:T(8,128)(2,1)} %weights_hbm.1, bf16[256,128]{1,0:T(8,128)(2,1)} %constant.16.clone.table_hbm, f32[4,1,2,128]{3,2,1,0:T(2,128)} %constant.17.clone.turn_hbm), custom_call_target="tpu_custom_call" | custom-call | tf_op jit(solution)/shard_map/mixing/pallas_call | solution.py:144
  1.9 6.3 %all-to-all-start = ((bf16[8,32,128]{2,1,0:T(8,128)(2,1)}), bf16[8,32,128]{2,1,0:T(8,128)(2,1)S(1)}, u32[]{:S(2)}, u32[]{:S(2)}) async-start(bf16[8,32,128]{2,1,0:T(8,128)(2,1)} %bitcast.2), calls=%async_computation | async-start | bytes 131072 | tf_op jit(solution)/shard_map/all_to_all | solution.py:321
  8.3 0.0 copy-start
  8.3 0.0 copy-start.1
  8.3 0.0 copy-start.2
  8.3 3.8 %range_forward.1.spec_ref = bf16[128,64,128]{2,1,0:T(8,128)(2,1)S(1)} custom-call(bf16[2,32,16384]{2,1,0:T(8,128)(2,1)} %pulses_hbm.1, f32[128,2,128]{2,1,0:T(2,128)} %bitcast.14, bf16[256,256]{1,0:T(8,128)(2,1)} %constant.18.clone.table_hbm, f32[2,128,128]{2,1,0:T(8,128)} %constant.19.clone.twist_hbm), custom_call_target="tpu_custom_call" | custom-call | flops 10000000000 | bytes 4194304 | tf_op jit(solution)/shard_map/range_forward/pallas_call | solution.py:233
  12.1 2.0 %all-to-all-done.mix_ref = bf16[8,32,128]{2,1,0:T(8,128)(2,1)S(1)} async-done(((bf16[8,32,128]{2,1,0:T(8,128)(2,1)}), bf16[8,32,128]{2,1,0:T(8,128)(2,1)S(1)}, u32[]{:S(2)}, u32[]{:S(2)}) %all-to-all-start) | async-done | bytes 65568 | tf_op jit(solution)/shard_map/all_to_all | solution.py:321
  14.2 0.0 copy-done
  14.2 0.0 copy-done.1
  14.2 0.0 copy-done.2
  14.2 2.2 %image_part.1 = (bf16[32,16,128]{2,1,0:T(8,128)(2,1)S(1)}, bf16[32,16,128]{2,1,0:T(8,128)(2,1)S(1)}) custom-call(bf16[128,64,128]{2,1,0:T(8,128)(2,1)S(1)} %range_forward.1.spec_ref, bf16[8,32,128]{2,1,0:T(8,128)(2,1)S(1)} %all-to-all-done.mix_ref, bf16[256,256]{1,0:T(8,128)(2,1)S(1)} %copy-done.1, f32[2,128,128]{2,1,0:T(8,128)S(1)} %copy-done, ...), custom_call_target="tpu_custom_call" | custom-call | tf_op jit(solution)/shard_map/image_part/pallas_call | solution.py:298
  16.4 0.1 collective-permute-start
  16.5 1.3 %collective-permute-done = bf16[32,16,128]{2,1,0:T(8,128)(2,1)S(1)} collective-permute-done((bf16[32,16,128]{2,1,0:T(8,128)(2,1)S(1)}, bf16[32,16,128]{2,1,0:T(8,128)(2,1)S(1)}, u32[]{:S(2)}, u32[]{:S(2)}) %collective-permute-start) | collective-permute-done | bytes 131104 | tf_op jit(solution)/shard_map/ppermute | solution.py:326
  17.8 12.0 %all_to_all.10 = bf16[32,16,128]{2,1,0:T(8,128)(2,1)S(1)} all-to-all(bf16[32,16,128]{2,1,0:T(8,128)(2,1)S(1)} %add_convert_fusion), channel_id=1, replica_groups=mesh['ang'=4,'pul'=8] {'ang','pul'}, dimensions={0} | all-to-all | bytes 262144 | tf_op jit(solution)/shard_map/all_to_all | solution.py:328
  29.8 0.6 %convert_reduce_fusion = f32[32,128]{1,0:T(8,128)} fusion(bf16[16,32,128]{2,1,0:T(8,128)(2,1)S(1)} %bitcast.13), kind=kLoop, calls=%fused_computation | loop fusion | flops 126976 | bytes 147456 | tf_op jit(solution)/shard_map/reduce_sum | solution.py:329
  (1 shorter events, 0.0 us)
Async XLA Ops:
  1.9 12.3 %all-to-all-start = ((bf16[8,32,128]{2,1,0:T(8,128)(2,1)}), bf16[8,32,128]{2,1,0:T(8,128)(2,1)S(1)}, u32[]{:S(2)}, u32[]{:S(2)}) async-start(bf16[8,32,128]{2,1,0:T(8,128)(2,1)} %bitcast.2), calls=%async_computation | async-start | bytes 131072 | tf_op jit(solution)/shard_map/all_to_all | solution.py:321
  8.3 5.9 %copy-start = (f32[2,128,128]{2,1,0:T(8,128)S(1)}, f32[2,128,128]{2,1,0:T(8,128)}, u32[]{:S(2)}) copy-start(f32[2,128,128]{2,1,0:T(8,128)} %constant.21.clone.twist_ref) | copy-start | bytes 393220
  8.3 5.9 %copy-start.1 = (bf16[256,256]{1,0:T(8,128)(2,1)S(1)}, bf16[256,256]{1,0:T(8,128)(2,1)}, u32[]{:S(2)}) copy-start(bf16[256,256]{1,0:T(8,128)(2,1)} %constant.20.clone.table_ref) | copy-start | bytes 393220
  8.3 5.9 %copy-start.2 = (bf16[32,256]{1,0:T(8,128)(2,1)S(1)}, bf16[32,256]{1,0:T(8,128)(2,1)}, u32[]{:S(2)}) copy-start(bf16[32,256]{1,0:T(8,128)(2,1)} %constant.22.clone.last_ref) | copy-start | bytes 49156
  16.4 1.4 %collective-permute-start = (bf16[32,16,128]{2,1,0:T(8,128)(2,1)S(1)}, bf16[32,16,128]{2,1,0:T(8,128)(2,1)S(1)}, u32[]{:S(2)}, u32[]{:S(2)}) collective-permute-start(bf16[32,16,128]{2,1,0:T(8,128)(2,1)S(1)} %get-tuple-element.8), channel_id=1, source_target_pairs={{0,1},{1,0},{2,3},{3,2},{4,5},{5,4},{6,7},{7,6},{8,9},{9,8},{10,11... | collective-permute-start | bytes 393224 | tf_op jit(solution)/shard_map/ppermute | solution.py:326

commit v5 on v4

--- a/solution.py
+++ b/solution.py
@@ -91,7 +91,7 @@
 
 
 def mixing_kernel(
-    blocks, chunks, offsets_hbm, weights_hbm, table_hbm, turn_hbm, out_ref,
+    blocks, chunks, offsets_hbm, weights_hbm, table_hbm, turn_hbm, pulses_hbm, out_ref, real_ref,
     offsets_ref, weights_ref, table_ref, turn_ref, product_ref, total_ref, sems,
 ):
     width = 4 * CHUNK
@@ -101,10 +101,11 @@
             (table_hbm, table_ref),
             (offsets_hbm, offsets_ref),
             (turn_hbm.at[lax.axis_index("ang")], turn_ref),
+            (pulses_hbm.at[0], real_ref),
         ],
         sems,
     )
-    for copy in copies:
+    for copy in copies[:4]:
         copy.wait()
     weights = weights_ref[...]
     column = lax.broadcasted_iota(jnp.int32, weights.shape, 1) // BLOCK_ROWS
@@ -136,16 +137,20 @@
         make(0)
     else:
         pl.loop(0, chunks)(make)
-
-
-def mixing(offsets, weights, table, turn):
+    copies[4].wait()
+
+
+def mixing(offsets, weights, table, turn, pulses):
     group_pulses, width = weights.shape[3], 4 * CHUNK
     chunks, blocks = table.shape[1] // width, offsets.shape[2]
     return pl.pallas_call(
         functools.partial(mixing_kernel, blocks, chunks),
-        out_shape=jax.ShapeDtypeStruct((group_pulses, chunks * width), BF),
-        in_specs=[HBM] * 4,
-        out_specs=VMEM,
+        out_shape=[
+            jax.ShapeDtypeStruct((group_pulses, chunks * width), BF),
+            jax.ShapeDtypeStruct(pulses.shape[1:], BF),
+        ],
+        in_specs=[HBM] * 5,
+        out_specs=[VMEM, VMEM],
         scratch_shapes=[
             pltpu.SMEM(offsets.shape, jnp.int32),
             pltpu.VMEM(weights.shape[2:], BF),
@@ -153,11 +158,11 @@
             pltpu.VMEM(turn.shape[1:], F32),
             pltpu.VMEM((blocks, BAND_PULSES, width), F32),
             pltpu.VMEM((group_pulses, width), F32),
-            pltpu.SemaphoreType.DMA((4,)),
+            pltpu.SemaphoreType.DMA((5,)),
         ],
         compiler_params=pltpu.CompilerParams(vmem_limit_bytes=24 * 2**20),
         name="mixing",
-    )(*in_hbm(offsets, weights, table, turn))
+    )(*in_hbm(offsets, weights, table, turn, pulses))
 
 
 def turn_by(wave, j, twist_ref):
@@ -172,24 +177,25 @@
 
 
 def range_kernel(
-    rows, pulses_hbm, filter_hbm, table_hbm, twist_hbm, out_ref,
-    pulses_ref, filter_ref, table_ref, twist_ref, wide_ref, spec_ref, sems,
+    rows, real_ref, pulses_hbm, filter_hbm, table_hbm, twist_hbm, out_ref,
+    imag_ref, filter_ref, table_ref, twist_ref, wide_ref, spec_ref, sems,
 ):
-    parts = 8
+    parts = 4
     length = FACTOR // parts
     pieces = [
-        (pulses_hbm.at[:, :, pl.ds(h * length * FACTOR, length * FACTOR)], pulses_ref.at[h]) for h in range(parts)
+        (pulses_hbm.at[1, :, pl.ds(h * length * FACTOR, length * FACTOR)], imag_ref.at[h]) for h in range(parts)
     ]
     copies = fetch(
         pieces + [(table_hbm, table_ref), (twist_hbm, twist_ref), (filter_hbm, filter_ref)], sems
     )
+    for m in range(FACTOR):
+        wide_ref[0, pl.ds(m * (rows + PAD), rows), :] = real_ref[:, m * FACTOR : (m + 1) * FACTOR].astype(F32)
     for h in range(parts):
         copies[h].wait()
         for m in range(length):
-            for c in range(2):
-                wide_ref[c, pl.ds((h * length + m) * (rows + PAD), rows), :] = pulses_ref[
-                    h, c, :, m * FACTOR : (m + 1) * FACTOR
-                ].astype(F32)
+            wide_ref[1, pl.ds((h * length + m) * (rows + PAD), rows), :] = imag_ref[
+                h, :, m * FACTOR : (m + 1) * FACTOR
+            ].astype(F32)
     copies[parts].wait()
     copies[parts + 1].wait()
     pair = 2
@@ -227,16 +233,16 @@
     lax.fori_loop(0, FACTOR // 8, narrow, 0, unroll=UNROLL["out"])
 
 
-def range_forward(pulses, matched_filter, table, twist):
-    rows, parts = pulses.shape[1], 8
+def range_forward(real, pulses, matched_filter, table, twist):
+    rows, parts = pulses.shape[1], 4
     filters = matched_filter.reshape(2, FACTOR, FACTOR).transpose(1, 0, 2)
     return pl.pallas_call(
         functools.partial(range_kernel, rows),
         out_shape=jax.ShapeDtypeStruct((FACTOR, 2 * rows, FACTOR), BF),
-        in_specs=[HBM] * 4,
+        in_specs=[VMEM] + [HBM] * 4,
         out_specs=VMEM,
         scratch_shapes=[
-            pltpu.VMEM((parts, 2, rows, FACTOR * FACTOR // parts), BF),
+            pltpu.VMEM((parts, rows, FACTOR * FACTOR // parts), BF),
             pltpu.VMEM((FACTOR, 2, FACTOR), F32),
             pltpu.VMEM((2 * FACTOR, 2 * FACTOR), BF),
             pltpu.VMEM((2, FACTOR, FACTOR), F32),
@@ -247,7 +253,7 @@
         compiler_params=pltpu.CompilerParams(vmem_limit_bytes=32 * 2**20),
         cost_estimate=pl.CostEstimate(flops=10**10, bytes_accessed=2**22, transcendentals=0),
         name="range_forward",
-    )(*in_hbm(pulses, filters, table, twist))
+    )(real, *in_hbm(pulses, filters, table, twist))
 
 
 def image_kernel(rows, tiles, spec_ref, mix_ref, table_ref, twist_ref, last_ref, keep_ref, give_ref, mixed_ref):
@@ -317,11 +323,11 @@
     pul_count, ang_count = lax.axis_size("pul"), lax.axis_size("ang")
     image_rows, rows = pul_count * ang_count, pulses.shape[1]
     azimuth, turn = azimuth_tables(image_rows, rows * pul_count, ang_count)
-    mix = mixing(offsets, interp_weights, azimuth, turn)
+    mix, real = mixing(offsets, interp_weights, azimuth, turn, pulses)
     mix = lax.all_to_all(
         mix.reshape(pul_count, rows, mix.shape[1]), "pul", split_axis=0, concat_axis=0, tiled=True
     )
-    spec = range_forward(pulses, matched_filter, *range_tables())
+    spec = range_forward(real, pulses, matched_filter, *range_tables())
     keep, give = image_part(spec, mix, *image_tables())
     got = lax.ppermute(give, "pul", [(i, i ^ 1) for i in range(pul_count)])
     part = (keep.astype(F32) + got.astype(F32)).astype(BF)

time: 30.8 us -> 30.4 us (0.987)
  waiting for transfers between devices: 3.38 us -> 3.73 us
    all_to_all x1, blocking collectives: 12 us -> 11.7 us  [local(): lax.all_to_all(part, ('ang', 'pul'), split_axis=0, concat_axis=0, tiled=T...]
    all_to_all x1, waiting for transfers between devices: 2.05 us -> 2.4 us  [local(): lax.all_to_all(mix.reshape(pul_count, rows, mix.shape[1]), 'pul', split_a...]
    pallas_call x1, Pallas kernels: 3.83 us -> 3.48 us  [range_forward(): pl.pallas_call(functools.partial(range_kernel, rows), out_shape=jax.Shape...]
  transfers between devices with their start and end apart: 2 -> 2, of which waited for: 2 -> 2; matrix products, arithmetic and copies ran while one was open for 0% -> 0% of each run, Pallas kernels for 13% -> 12%
where the time goes in v5:
time: 30.4 us; the launch traced here: 30.2 us
  blocking collectives  11.7 us (38%)
  Pallas kernels  7.64 us (25%)
  starting transfers between devices  6.41 us (21%)
  waiting for transfers between devices  3.73 us (12%)
  other arithmetic  0.66 us (2%)
    all_to_all x1, blocking collectives, local(): lax.all_to_all(part, ('ang', 'pul'), split_axis=0, concat_axis=0, tiled=T...  11.7 us
    all_to_all x1, starting transfers between devices, local(): lax.all_to_all(mix.reshape(pul_count, rows, mix.shape[1]), 'pul', split_a...  6.34 us
    pallas_call x1, Pallas kernels, range_forward(): pl.pallas_call(functools.partial(range_kernel, rows), out_shape=jax.Shape...  3.48 us
    all_to_all x1, waiting for transfers between devices, local(): lax.all_to_all(mix.reshape(pul_count, rows, mix.shape[1]), 'pul', split_a...  2.4 us
    pallas_call x1, Pallas kernels, image_part(): pl.pallas_call(functools.partial(image_kernel, rows, tiles), grid=(chunks...  2.21 us
    pallas_call x1, Pallas kernels, mixing(): pl.pallas_call(functools.partial(mixing_kernel, blocks, chunks), out_shap...  1.96 us
    ppermute x1, waiting for transfers between devices, local(): got = lax.ppermute(give, 'pul', [(i, i ^ 1) for i in range(pul_count)])  1.33 us
    reduce_sum x1, other arithmetic, local(): jnp.sum(parts.reshape(image_rows // 2, -1, FACTOR).astype(F32), axis=0)  0.63 us
  transfers between devices with their start and end apart: 2, of which 2 were waited for; matrix products, arithmetic and copies ran while one was open for 0% of the time, Pallas kernels for 12%

profile of v5, /device:TPU:0, one launch (start us, length us, event | category | flops | bytes accessed | tf_op | source)
XLA Modules:
  0.0 30.2 jit_solution(9543189543134458525)
XLA Ops:
  0.0 2.0 %mixing.1 = (bf16[256,128]{1,0:T(8,128)(2,1)}, bf16[32,16384]{1,0:T(8,128)(2,1)S(1)}) custom-call(s32[1,1,8]{2,1,0:T(1,128)} %offsets_hbm.1, bf16[1,1,64,256]{3,2,1,0:T(8,128)(2,1)} %weights_hbm.1, bf16[256,128]{1,0:T(8,128)(2,1)} %constant.16.clone.table_hbm, f32[4,1,2,128]{3,2,1,0:T(2,128)} %constant.17.clone.turn_hbm, bf16[2,32,16384]{2,1,0:T(8,128)(2,1)} %pulses_hbm.3), custom_call_target="tpu_custom_call" | custom-call | tf_op jit(solution)/shard_map/mixing/pallas_call | solution.py:146
  2.0 6.3 %all-to-all-start = ((bf16[8,32,128]{2,1,0:T(8,128)(2,1)}), bf16[8,32,128]{2,1,0:T(8,128)(2,1)S(1)}, u32[]{:S(2)}, u32[]{:S(2)}) async-start(bf16[8,32,128]{2,1,0:T(8,128)(2,1)} %bitcast.2), calls=%async_computation | async-start | bytes 131072 | tf_op jit(solution)/shard_map/all_to_all | solution.py:327
  8.3 0.0 copy-start
  8.3 0.0 copy-start.1
  8.3 0.0 copy-start.2
  8.3 3.5 %range_forward.1.spec_ref = bf16[128,64,128]{2,1,0:T(8,128)(2,1)S(1)} custom-call(bf16[32,16384]{1,0:T(8,128)(2,1)S(1)} %get-tuple-element.9.real_ref, bf16[2,32,16384]{2,1,0:T(8,128)(2,1)} %pulses_hbm.3, f32[128,2,128]{2,1,0:T(2,128)} %bitcast.14, bf16[256,256]{1,0:T(8,128)(2,1)} %constant.18.clone.table_hbm, f32[2,128,128]{2,1,0:T(8,128)} %constant.19.clone.twist_hbm), custom_call_target="tpu_custom_call" | custom-call | flops 10000000000 | bytes 4194304 | tf_op jit(solution)/shard_map/range_forward/pallas_call | solution.py:239
  11.8 2.4 %all-to-all-done.mix_ref = bf16[8,32,128]{2,1,0:T(8,128)(2,1)S(1)} async-done(((bf16[8,32,128]{2,1,0:T(8,128)(2,1)}), bf16[8,32,128]{2,1,0:T(8,128)(2,1)S(1)}, u32[]{:S(2)}, u32[]{:S(2)}) %all-to-all-start) | async-done | bytes 65568 | tf_op jit(solution)/shard_map/all_to_all | solution.py:327
  14.2 0.0 copy-done
  14.2 0.0 copy-done.1
  14.2 0.0 copy-done.2
  14.2 2.2 %image_part.1 = (bf16[32,16,128]{2,1,0:T(8,128)(2,1)S(1)}, bf16[32,16,128]{2,1,0:T(8,128)(2,1)S(1)}) custom-call(bf16[128,64,128]{2,1,0:T(8,128)(2,1)S(1)} %range_forward.1.spec_ref, bf16[8,32,128]{2,1,0:T(8,128)(2,1)S(1)} %all-to-all-done.mix_ref, bf16[256,256]{1,0:T(8,128)(2,1)S(1)} %copy-done.1, f32[2,128,128]{2,1,0:T(8,128)S(1)} %copy-done, ...), custom_call_target="tpu_custom_call" | custom-call | tf_op jit(solution)/shard_map/image_part/pallas_call | solution.py:304
  16.4 0.1 collective-permute-start
  16.5 1.3 %collective-permute-done = bf16[32,16,128]{2,1,0:T(8,128)(2,1)S(1)} collective-permute-done((bf16[32,16,128]{2,1,0:T(8,128)(2,1)S(1)}, bf16[32,16,128]{2,1,0:T(8,128)(2,1)S(1)}, u32[]{:S(2)}, u32[]{:S(2)}) %collective-permute-start) | collective-permute-done | bytes 131104 | tf_op jit(solution)/shard_map/ppermute | solution.py:332
  17.9 11.7 %all_to_all.10 = bf16[32,16,128]{2,1,0:T(8,128)(2,1)S(1)} all-to-all(bf16[32,16,128]{2,1,0:T(8,128)(2,1)S(1)} %add_convert_fusion), channel_id=1, replica_groups=mesh['ang'=4,'pul'=8] {'ang','pul'}, dimensions={0} | all-to-all | bytes 262144 | tf_op jit(solution)/shard_map/all_to_all | solution.py:334
  29.5 0.6 %convert_reduce_fusion = f32[32,128]{1,0:T(8,128)} fusion(bf16[16,32,128]{2,1,0:T(8,128)(2,1)S(1)} %bitcast.13), kind=kLoop, calls=%fused_computation | loop fusion | flops 126976 | bytes 147456 | tf_op jit(solution)/shard_map/reduce_sum | solution.py:335
  (1 shorter events, 0.0 us)
Async XLA Ops:
  2.0 12.3 %all-to-all-start = ((bf16[8,32,128]{2,1,0:T(8,128)(2,1)}), bf16[8,32,128]{2,1,0:T(8,128)(2,1)S(1)}, u32[]{:S(2)}, u32[]{:S(2)}) async-start(bf16[8,32,128]{2,1,0:T(8,128)(2,1)} %bitcast.2), calls=%async_computation | async-start | bytes 131072 | tf_op jit(solution)/shard_map/all_to_all | solution.py:327
  8.3 5.9 %copy-start = (f32[2,128,128]{2,1,0:T(8,128)S(1)}, f32[2,128,128]{2,1,0:T(8,128)}, u32[]{:S(2)}) copy-start(f32[2,128,128]{2,1,0:T(8,128)} %constant.21.clone.twist_ref) | copy-start | bytes 393220
  8.3 5.9 %copy-start.1 = (bf16[256,256]{1,0:T(8,128)(2,1)S(1)}, bf16[256,256]{1,0:T(8,128)(2,1)}, u32[]{:S(2)}) copy-start(bf16[256,256]{1,0:T(8,128)(2,1)} %constant.20.clone.table_ref) | copy-start | bytes 393220
  8.3 5.9 %copy-start.2 = (bf16[32,256]{1,0:T(8,128)(2,1)S(1)}, bf16[32,256]{1,0:T(8,128)(2,1)}, u32[]{:S(2)}) copy-start(bf16[32,256]{1,0:T(8,128)(2,1)} %constant.22.clone.last_ref) | copy-start | bytes 49156
  16.4 1.4 %collective-permute-start = (bf16[32,16,128]{2,1,0:T(8,128)(2,1)S(1)}, bf16[32,16,128]{2,1,0:T(8,128)(2,1)S(1)}, u32[]{:S(2)}, u32[]{:S(2)}) collective-permute-start(bf16[32,16,128]{2,1,0:T(8,128)(2,1)S(1)} %get-tuple-element.12), channel_id=1, source_target_pairs={{0,1},{1,0},{2,3},{3,2},{4,5},{5,4},{6,7},{7,6},{8,9},{9,8},{10,11... | collective-permute-start | bytes 393224 | tf_op jit(solution)/shard_map/ppermute | solution.py:332

commit v6 on v5

--- a/solution.py
+++ b/solution.py
@@ -131,7 +131,11 @@
         turn = turn_ref[chunk]
         total = total_ref[...]
         other = pltpu.roll(total, width // 2, 1)
-        out_ref[:, columns] = (total * turn[0:1] + other * turn[1:2]).astype(BF)
+        mixed = total * turn[0:1] + other * turn[1:2]
+        lower = mixed.reshape(-1, 2, 16, width)[:, 0]
+        upper = pltpu.roll(mixed, width // 2, 1).reshape(-1, 2, 16, width)[:, 1]
+        lane = lax.broadcasted_iota(jnp.int32, lower.shape, 2)
+        out_ref[:, columns] = jnp.where(lane < width // 2, lower, upper).reshape(-1, width).astype(BF)
 
     if chunks == 1:
         make(0)
@@ -146,7 +150,7 @@
     return pl.pallas_call(
         functools.partial(mixing_kernel, blocks, chunks),
         out_shape=[
-            jax.ShapeDtypeStruct((group_pulses, chunks * width), BF),
+            jax.ShapeDtypeStruct((group_pulses // 2, chunks * width), BF),
             jax.ShapeDtypeStruct(pulses.shape[1:], BF),
         ],
         in_specs=[HBM] * 5,
@@ -260,7 +264,9 @@
     wide = 2 * CHUNK
     for t in range(tiles):
         mix = mix_ref[t].astype(F32)
-        mix = jnp.concatenate([mix[:, :wide], mix[:, wide:]], axis=0).T.astype(BF)
+        mix = jnp.concatenate([mix[:, :wide], mix[:, wide:]], axis=0)
+        turned = jnp.concatenate([-mix[:, CHUNK:], mix[:, :CHUNK]], axis=1)
+        mix = jnp.concatenate([mix, turned], axis=0).T.astype(BF)
         for k2 in range(t * (FACTOR // tiles), (t + 1) * (FACTOR // tiles)):
             mixed_ref[pl.ds(k2 * (wide + PAD), wide), :] = jnp.dot(mix, spec_ref[k2], preferred_element_type=F32)
     pair = 2
@@ -325,7 +331,7 @@
     azimuth, turn = azimuth_tables(image_rows, rows * pul_count, ang_count)
     mix, real = mixing(offsets, interp_weights, azimuth, turn, pulses)
     mix = lax.all_to_all(
-        mix.reshape(pul_count, rows, mix.shape[1]), "pul", split_axis=0, concat_axis=0, tiled=True
+        mix.reshape(pul_count, rows // 2, mix.shape[1]), "pul", split_axis=0, concat_axis=0, tiled=True
     )
     spec = range_forward(real, pulses, matched_filter, *range_tables())
     keep, give = image_part(spec, mix, *image_tables())

time: 30.4 us -> 30.6 us (level)
  transfers between devices with their start and end apart: 2 -> 2, of which waited for: 2 -> 2; matrix products, arithmetic and copies ran while one was open for 0% -> 0% of each run, Pallas kernels for 12% -> 11%
where the time goes in v6:
time: 30.6 us; the launch traced here: 30.3 us
  blocking collectives  11.8 us (39%)
  Pallas kernels  7.8 us (25%)
  starting transfers between devices  6.41 us (21%)
  waiting for transfers between devices  3.56 us (12%)
  other arithmetic  0.66 us (2%)
    all_to_all x1, blocking collectives, local(): lax.all_to_all(part, ('ang', 'pul'), split_axis=0, concat_axis=0, tiled=T...  11.8 us
    all_to_all x1, starting transfers between devices, local(): lax.all_to_all(mix.reshape(pul_count, rows // 2, mix.shape[1]), 'pul', sp...  6.34 us
    pallas_call x1, Pallas kernels, range_forward(): pl.pallas_call(functools.partial(range_kernel, rows), out_shape=jax.Shape...  3.48 us
    pallas_call x1, Pallas kernels, image_part(): pl.pallas_call(functools.partial(image_kernel, rows, tiles), grid=(chunks...  2.37 us
    all_to_all x1, waiting for transfers between devices, local(): lax.all_to_all(mix.reshape(pul_count, rows // 2, mix.shape[1]), 'pul', sp...  2.22 us
    pallas_call x1, Pallas kernels, mixing(): pl.pallas_call(functools.partial(mixing_kernel, blocks, chunks), out_shap...  1.96 us
    ppermute x1, waiting for transfers between devices, local(): got = lax.ppermute(give, 'pul', [(i, i ^ 1) for i in range(pul_count)])  1.33 us
    reduce_sum x1, other arithmetic, local(): jnp.sum(parts.reshape(image_rows // 2, -1, FACTOR).astype(F32), axis=0)  0.63 us
  transfers between devices with their start and end apart: 2, of which 2 were waited for; matrix products, arithmetic and copies ran while one was open for 0% of the time, Pallas kernels for 11%

profile of v6, /device:TPU:0, one launch (start us, length us, event | category | flops | bytes accessed | tf_op | source)
XLA Modules:
  0.0 30.3 jit_solution(17750642643971558605)
XLA Ops:
  0.0 2.0 %mixing.1 = (bf16[128,128]{1,0:T(8,128)(2,1)}, bf16[32,16384]{1,0:T(8,128)(2,1)S(1)}) custom-call(s32[1,1,8]{2,1,0:T(1,128)} %offsets_hbm.1, bf16[1,1,64,256]{3,2,1,0:T(8,128)(2,1)} %weights_hbm.1, bf16[256,128]{1,0:T(8,128)(2,1)} %constant.16.clone.table_hbm, f32[4,1,2,128]{3,2,1,0:T(2,128)} %constant.17.clone.turn_hbm, bf16[2,32,16384]{2,1,0:T(8,128)(2,1)} %pulses_hbm.3), custom_call_target="tpu_custom_call" | custom-call | tf_op jit(solution)/shard_map/mixing/pallas_call | solution.py:150
  2.0 6.3 %all-to-all-start = ((bf16[8,16,128]{2,1,0:T(8,128)(2,1)}), bf16[8,16,128]{2,1,0:T(8,128)(2,1)S(1)}, u32[]{:S(2)}, u32[]{:S(2)}) async-start(bf16[8,16,128]{2,1,0:T(8,128)(2,1)} %bitcast.2), calls=%async_computation | async-start | bytes 65536 | tf_op jit(solution)/shard_map/all_to_all | solution.py:333
  8.3 0.0 copy-start
  8.3 0.0 copy-start.1
  8.3 0.0 copy-start.2
  8.3 3.5 %range_forward.1.spec_ref = bf16[128,64,128]{2,1,0:T(8,128)(2,1)S(1)} custom-call(bf16[32,16384]{1,0:T(8,128)(2,1)S(1)} %get-tuple-element.9.real_ref, bf16[2,32,16384]{2,1,0:T(8,128)(2,1)} %pulses_hbm.3, f32[128,2,128]{2,1,0:T(2,128)} %bitcast.14, bf16[256,256]{1,0:T(8,128)(2,1)} %constant.18.clone.table_hbm, f32[2,128,128]{2,1,0:T(8,128)} %constant.19.clone.twist_hbm), custom_call_target="tpu_custom_call" | custom-call | flops 10000000000 | bytes 4194304 | tf_op jit(solution)/shard_map/range_forward/pallas_call | solution.py:243
  11.8 2.2 %all-to-all-done.mix_ref = bf16[8,16,128]{2,1,0:T(8,128)(2,1)S(1)} async-done(((bf16[8,16,128]{2,1,0:T(8,128)(2,1)}), bf16[8,16,128]{2,1,0:T(8,128)(2,1)S(1)}, u32[]{:S(2)}, u32[]{:S(2)}) %all-to-all-start) | async-done | bytes 32800 | tf_op jit(solution)/shard_map/all_to_all | solution.py:333
  14.0 0.0 copy-done
  14.0 0.0 copy-done.1
  14.0 0.0 copy-done.2
  14.1 2.4 %image_part.1 = (bf16[32,16,128]{2,1,0:T(8,128)(2,1)S(1)}, bf16[32,16,128]{2,1,0:T(8,128)(2,1)S(1)}) custom-call(bf16[128,64,128]{2,1,0:T(8,128)(2,1)S(1)} %range_forward.1.spec_ref, bf16[8,16,128]{2,1,0:T(8,128)(2,1)S(1)} %all-to-all-done.mix_ref, bf16[256,256]{1,0:T(8,128)(2,1)S(1)} %copy-done.1, f32[2,128,128]{2,1,0:T(8,128)S(1)} %copy-done, ...), custom_call_target="tpu_custom_call" | custom-call | tf_op jit(solution)/shard_map/image_part/pallas_call | solution.py:310
  16.4 0.1 collective-permute-start
  16.5 1.3 %collective-permute-done = bf16[32,16,128]{2,1,0:T(8,128)(2,1)S(1)} collective-permute-done((bf16[32,16,128]{2,1,0:T(8,128)(2,1)S(1)}, bf16[32,16,128]{2,1,0:T(8,128)(2,1)S(1)}, u32[]{:S(2)}, u32[]{:S(2)}) %collective-permute-start) | collective-permute-done | bytes 131104 | tf_op jit(solution)/shard_map/ppermute | solution.py:338
  17.9 11.8 %all_to_all.10 = bf16[32,16,128]{2,1,0:T(8,128)(2,1)S(1)} all-to-all(bf16[32,16,128]{2,1,0:T(8,128)(2,1)S(1)} %add_convert_fusion), channel_id=1, replica_groups=mesh['ang'=4,'pul'=8] {'ang','pul'}, dimensions={0} | all-to-all | bytes 262144 | tf_op jit(solution)/shard_map/all_to_all | solution.py:340
  29.7 0.6 %convert_reduce_fusion = f32[32,128]{1,0:T(8,128)} fusion(bf16[16,32,128]{2,1,0:T(8,128)(2,1)S(1)} %bitcast.13), kind=kLoop, calls=%fused_computation | loop fusion | flops 126976 | bytes 147456 | tf_op jit(solution)/shard_map/reduce_sum | solution.py:341
  (1 shorter events, 0.0 us)
Async XLA Ops:
  2.0 12.1 %all-to-all-start = ((bf16[8,16,128]{2,1,0:T(8,128)(2,1)}), bf16[8,16,128]{2,1,0:T(8,128)(2,1)S(1)}, u32[]{:S(2)}, u32[]{:S(2)}) async-start(bf16[8,16,128]{2,1,0:T(8,128)(2,1)} %bitcast.2), calls=%async_computation | async-start | bytes 65536 | tf_op jit(solution)/shard_map/all_to_all | solution.py:333
  8.3 5.7 %copy-start = (f32[2,128,128]{2,1,0:T(8,128)S(1)}, f32[2,128,128]{2,1,0:T(8,128)}, u32[]{:S(2)}) copy-start(f32[2,128,128]{2,1,0:T(8,128)} %constant.21.clone.twist_ref) | copy-start | bytes 393220
  8.3 5.7 %copy-start.1 = (bf16[256,256]{1,0:T(8,128)(2,1)S(1)}, bf16[256,256]{1,0:T(8,128)(2,1)}, u32[]{:S(2)}) copy-start(bf16[256,256]{1,0:T(8,128)(2,1)} %constant.20.clone.table_ref) | copy-start | bytes 393220
  8.3 5.7 %copy-start.2 = (bf16[32,256]{1,0:T(8,128)(2,1)S(1)}, bf16[32,256]{1,0:T(8,128)(2,1)}, u32[]{:S(2)}) copy-start(bf16[32,256]{1,0:T(8,128)(2,1)} %constant.22.clone.last_ref) | copy-start | bytes 49156
  16.4 1.4 %collective-permute-start = (bf16[32,16,128]{2,1,0:T(8,128)(2,1)S(1)}, bf16[32,16,128]{2,1,0:T(8,128)(2,1)S(1)}, u32[]{:S(2)}, u32[]{:S(2)}) collective-permute-start(bf16[32,16,128]{2,1,0:T(8,128)(2,1)S(1)} %get-tuple-element.12), channel_id=1, source_target_pairs={{0,1},{1,0},{2,3},{3,2},{4,5},{5,4},{6,7},{7,6},{8,9},{9,8},{10,11... | collective-permute-start | bytes 393224 | tf_op jit(solution)/shard_map/ppermute | solution.py:338
